TPU v7x, 32 devices: a whole 2x2x4 slice. The times are simulated.
32 devices in a mesh: dp: 4 (over y, core), seq: 8 (over z, x).
Axes of the slice: x: 2, y: 2, z: 4, core: 2. Of those that a mesh axis runs over, the one named last changes fastest.
Arguments:
- queries: bfloat16 [8, 512, 1536], P('dp', 'seq'), may hold values from -6 to 6
- key_rows: bfloat16 [8, 512, 1536], P('dp', 'seq'), may hold values from -6 to 6
- value_rows: bfloat16 [8, 512, 1536], P('dp', 'seq'), may hold values from -6 to 6
- layer_input: bfloat16 [8, 512, 1536], P('dp', 'seq'), may hold values from -6 to 6
- utt_lengths: int32 [8], P('dp'), may hold values from 128 to 512, as said below
- out_weight: bfloat16 [1536, 1536], replicated, may hold values from -0.15625 to 0.15625
- conv_kernel: bfloat16 [31, 1536], replicated, may hold values from -1 to 1
- conv_cotangent: bfloat16 [8, 512, 1536], P('dp', 'seq'), may hold values from -6 to 6
- pick_weight: int32 [23592], replicated, may hold values from 0 to 2359295
- pick_kernel: int32 [476], replicated, may hold values from 0 to 47615
Outputs:
- conv_out: bfloat16 [8, 512, 1536], P('dp', 'seq')
- context_grad: bfloat16 [8, 512, 1536], P('dp', 'seq')
- weight_picks: float32 [23592], replicated
- kernel_picks: float32 [476], replicated
Inputs may be any that keep to these rules, and one draw needn't show every extreme that they name: `utt_lengths`: the first utterance fills all 512 slots and the last has 128 valid frames.
All inputs are finite; a program needn't handle non-finite values.
Results may differ from a plain program's by a relative error of at most 0.0056.
Values may be sent and summed in bfloat16 or wider, within the bound.
A program may use at most 128 MiB of HBM per device.

v0:
```python
import math

import jax
import jax.numpy as jnp
from jax import lax
from jax.sharding import PartitionSpec as P

HEADS = 16


neg_big = -1e30


def padded(value, sides, width):
    for axis, dim in sides:
        count, length = (lax.axis_size(axis), value.shape[dim])
        up = [(i, (i + 1) % count) for i in range(count - 1)]
        down = [(j, i) for i, j in up]
        last = lax.slice_in_dim(value, length - width, length, axis=dim)
        leading = lax.slice_in_dim(value, 0, width, axis=dim)
        before = lax.ppermute(last, axis, up)
        after = lax.ppermute(leading, axis, down)
        value = jnp.concatenate([before, value, after], axis=dim)
    return value


def softmax_rows(scores, key_ok):
    scores = jnp.where(key_ok, scores, neg_big)
    row_max = jnp.max(scores, axis=-1, keepdims=True)
    probs = jnp.exp(scores - row_max)
    return (probs.astype(jnp.bfloat16), jnp.sum(probs, axis=-1))


def pick_entries(table, picks):
    flat = table.reshape(-1)
    lane = math.gcd(flat.shape[0], 128)
    blocks = flat.reshape(flat.shape[0] // lane, lane)
    chosen = jnp.take(blocks, picks // lane, axis=0)
    lane_ids = jnp.arange(lane, dtype=jnp.int32)
    hit = lane_ids[None, :] == (picks % lane)[:, None]
    return jnp.sum(jnp.where(hit, chosen, jnp.float32(0.0)), axis=1)


def on_device(
    queries,
    key_rows,
    value_rows,
    layer_input,
    utt_lengths,
    out_weight,
    conv_kernel,
    conv_cotangent,
    pick_weight,
    pick_kernel,
):
    local_utts, frames_dev, width = queries.shape
    seq_count = lax.axis_size("seq")
    full_frames = frames_dev * seq_count
    head_size = width // HEADS
    score_scale = 1.0 / math.sqrt(head_size)
    first_frame = lax.axis_index("seq") * frames_dev
    local_ids = first_frame + jnp.arange(frames_dev, dtype=jnp.int32)
    valid_rows = (local_ids[None, :] < utt_lengths[:, None]).astype(jnp.float32)
    all_keys, all_values = (
        lax.all_gather(key_rows, "seq", axis=1, tiled=True),
        lax.all_gather(value_rows, "seq", axis=1, tiled=True),
    )
    full_ids = jnp.arange(full_frames, dtype=jnp.int32)

    def one_utt(item):
        query_utt, key_utt, value_utt, length_utt = item
        query_heads = query_utt.reshape(frames_dev, HEADS, head_size)
        key_heads = key_utt.reshape(full_frames, HEADS, head_size)
        value_heads = value_utt.reshape(full_frames, HEADS, head_size)
        scores = (
            jnp.einsum("qhd,khd->hqk", query_heads, key_heads, preferred_element_type=jnp.float32)
            * score_scale
        )
        weights, denom = softmax_rows(scores, (full_ids < length_utt)[None, None, :])
        out_rows = jnp.einsum(
            "hqk,khd->qhd", weights, value_heads, preferred_element_type=jnp.float32
        )
        out_rows = out_rows / denom.transpose(1, 0)[:, :, None]
        return out_rows.astype(jnp.bfloat16).reshape(frames_dev, width)

    context = lax.map(one_utt, (queries, all_keys, all_values, utt_lengths))
    context_flat = context.reshape(local_utts * frames_dev, width)
    projected = jnp.dot(context_flat, out_weight, preferred_element_type=jnp.float32).reshape(
        local_utts, frames_dev, width
    )
    hidden = ((layer_input.astype(jnp.float32) + projected) * valid_rows[:, :, None]).astype(
        jnp.bfloat16
    )
    tap_count = conv_kernel.shape[0]
    half_taps = (tap_count - 1) // 2
    kernel_f = conv_kernel.astype(jnp.float32)
    hidden_pad = padded(hidden, (("seq", 1),), half_taps)
    cot_f = conv_cotangent.astype(jnp.float32)
    conv_sum = jnp.zeros((local_utts, frames_dev, width), jnp.float32)
    kernel_rows = []
    for offset in range(tap_count):
        window = hidden_pad[:, offset : offset + frames_dev].astype(jnp.float32)
        conv_sum = conv_sum + kernel_f[offset] * window
        kernel_rows.append(jnp.sum(window * cot_f, axis=(0, 1)))
    conv_out = conv_sum.astype(jnp.bfloat16)
    kernel_grad = jnp.stack(kernel_rows)
    cot_pad = padded(conv_cotangent, (("seq", 1),), half_taps).astype(jnp.float32)
    back_sum = jnp.zeros((local_utts, frames_dev, width), jnp.float32)
    for offset in range(tap_count):
        begin = 2 * half_taps - offset
        back_sum = back_sum + kernel_f[offset] * cot_pad[:, begin : begin + frames_dev]
    hidden_grad = (back_sum * valid_rows[:, :, None]).astype(jnp.bfloat16)
    grad_flat = hidden_grad.reshape(local_utts * frames_dev, width)
    weight_grad = lax.dot_general(
        context_flat, grad_flat, (((0,), (0,)), ((), ())), preferred_element_type=jnp.float32
    )
    context_grad = lax.dot_general(
        grad_flat, out_weight, (((1,), (1,)), ((), ())), preferred_element_type=jnp.float32
    )
    context_grad = context_grad.reshape(local_utts, frames_dev, width).astype(jnp.bfloat16)
    weight_vals = pick_entries(weight_grad, pick_weight)
    kernel_vals = pick_entries(kernel_grad, pick_kernel)
    weight_sum, kernel_sum = lax.psum((weight_vals, kernel_vals), ("dp", "seq"))
    total_slots = local_utts * lax.axis_size("dp") * full_frames
    norm_factor = 1.0 / math.sqrt(total_slots)
    return (conv_out, context_grad, weight_sum * norm_factor, kernel_sum * norm_factor)


def solution(mesh):
    placed = (
        P("dp", "seq", None),
        P("dp", "seq", None),
        P("dp", "seq", None),
        P("dp", "seq", None),
        P("dp"),
        P(),
        P(),
        P("dp", "seq", None),
        P(),
        P(),
    )
    return jax.shard_map(
        on_device,
        mesh=mesh,
        in_specs=placed,
        out_specs=(P("dp", "seq", None), P("dp", "seq", None), P(), P()),
        check_vma=False,
    )
```

profile of v0, /device:TPU:0, one launch (start us, length us, event | category | flops | bytes accessed | tf_op | source)
XLA Modules:
  0.0 438.3 jit_solution(12545101080541474624)
XLA Ops:
  7.3 2.2 copy.23
  9.5 0.0 all-gather.3.cloned.1.call-start
  9.5 2.2 copy.22
  11.8 4.8 %collective-permute-start.2 = (bf16[2,15,1536]{2,1,0:T(8,128)(2,1)S(1)}, bf16[2,15,1536]{2,1,0:T(8,128)(2,1)S(1)}, u32[]{:S(2)}, u32[]{:S(2)}) collective-permute-start(bf16[2,15,1536]{2,1,0:T(8,128)(2,1)S(1)} %get-tuple-element.144), channel_id=1, source_target_pairs={{0,1},{1,2},{2,3},{3,4},{4,5},{5,6},{6,7},{8,9},{9,10},{10,11},{11... | collective-permute-start | bytes 276488 | tf_op jit(solution)/shard_map/ppermute | solution.py:21
  16.7 1.3 collective-permute-start.3
  18.0 0.2 slice_reduce_fusion.29
  18.4 0.3 slice_reduce_fusion.30
  18.8 0.7 compare_convert_fusion
  19.6 0.6 add_select_fusion.3
  20.2 0.6 compare_and_fusion.1
  20.7 0.1 compare_and_fusion
  20.8 0.7 pad_clamp_fusion
  21.5 0.6 pad_clamp_fusion.1
  22.1 1.1 collective-permute-done.3
  23.2 0.2 maximum_convert_fusion
  23.4 3.1 fusion.96
  26.8 0.7 copy-done.2
  27.5 2.4 fusion.26
  29.9 43.4 %all-gather.5.cloned.1.call-done = bf16[2,512,1536]{2,0,1:T(2,128)(2,1)} async-done(((bf16[2,64,1536]{2,0,1:T(2,128)(2,1)}), bf16[2,512,1536]{2,0,1:T(2,128)(2,1)}) %all-gather.5.cloned.1.call-update) | async-done | bytes 3145744 | tf_op jit(solution)/shard_map/all_gather | solution.py:65
  73.4 7.0 %copy.25 = bf16[2,512,1536]{1,2,0:T(8,128)(2,1)S(1)} copy(bf16[2,512,1536]{2,0,1:T(2,128)(2,1)} %all-gather.5.cloned.1.call-done) | data formatting | bytes 6291456
  80.4 54.3 %all-gather.3.cloned.1.call-done = bf16[2,512,1536]{2,0,1:T(2,128)(2,1)} async-done(((bf16[2,64,1536]{2,0,1:T(2,128)(2,1)}), bf16[2,512,1536]{2,0,1:T(2,128)(2,1)}) %all-gather.3.cloned.1.call-update) | async-done | bytes 3145744 | tf_op jit(solution)/shard_map/all_gather | solution.py:66
  134.6 8.6 %copy.24 = bf16[2,512,1536]{1,2,0:T(8,128)(2,1)} copy(bf16[2,512,1536]{2,0,1:T(2,128)(2,1)} %all-gather.3.cloned.1.call-done) | data formatting | bytes 6291456
  143.3 23.5 %while.11 = (s32[]{:T(128)}, bf16[2,64,1536]{2,1,0:T(8,128)(2,1)}, bf16[2,512,1536]{1,2,0:T(8,128)(2,1)}, s32[2]{0:T(128)}, bf16[2,64,1536]{2,1,0:T(8,128)(2,1)}, /*index=5*/bf16[2,512,1536]{1,2,0:T(8,128)(2,1)S(1)}, s32[]{:T(128)}) while((s32[]{:T(128)}, bf16[2,64,1536]{2,1,0:T(8,128)(2,1)}, bf16[2,512,1536]{1,2,0:T(8,128)(2,1)}, ...), condition=%wide.region_3.4_spmd.clone, body=%wide.region_0.3_spmd.clone.sunk | while | flops 207288832 | bytes 18112652 | solution.py:86
  143.3 1.3 dynamic_slice.27
  144.6 1.2 iota_compare_fusion.4
  145.7 1.6 constant_dynamic-slice_fusion.6
  147.3 1.2 reshape.166
  148.5 1.6 constant_dynamic-slice_fusion.5
  150.1 0.6 fusion.174
  150.7 0.6 fusion.175
  151.4 0.9 fusion.176
  152.3 0.2 copy.33
  152.5 0.9 broadcast_in_dim.105
  153.4 1.6 constant_dynamic-update-slice_fusion.2
  155.0 1.3 dynamic_slice.27
  156.3 1.2 iota_compare_fusion.4
  157.5 1.6 constant_dynamic-slice_fusion.6
  159.1 1.2 reshape.166
  160.2 1.6 constant_dynamic-slice_fusion.5
  161.9 0.6 fusion.174
  162.5 0.6 fusion.175
  163.1 0.9 fusion.176
  164.1 0.2 copy.33
  164.2 0.9 broadcast_in_dim.105
  165.2 1.6 constant_dynamic-update-slice_fusion.2
  166.8 6.2 %convolution_bitcast_fusion.1 = f32[1536,1536]{1,0:T(8,128)} fusion(bf16[2,64,1536]{2,1,0:T(8,128)(2,1)} %get-tuple-element.41, bf16[2,64,1536]{2,1,0:T(8,128)(2,1)} %copy-done.2), kind=kOutput, calls=%fused_computation.26 | convolution fusion | flops 603979776 | bytes 10223616 | tf_op jit(solution)/shard_map/dot_general | solution.py:114
  173.0 3.1 fusion.29
  176.2 10.6 %reshape_reshape.6 = f32[18432,128]{1,0:T(8,128)} reshape(f32[1536,1536]{1,0:T(8,128)} %convolution_bitcast_fusion.1) | data formatting | bytes 18874368 | tf_op jit(solution)/shard_map/reshape;reshape | solution.py:37
  186.7 47.9 %gather_fusion = f32[23592,128]{1,0:T(8,128)} fusion(f32[18432,128]{1,0:T(8,128)} %reshape_reshape.6, s32[24576]{0:T(1024)S(1)} %copy-done.4), kind=kCustom, calls=%fused_computation | custom fusion | bytes 24252576 | tf_op jit(solution)/shard_map/jit(_take)/gather | solution.py:38
  234.7 22.9 %select_reduce_fusion = f32[23592]{0:T(1024)} fusion(f32[23592,128]{1,0:T(8,128)} %gather_fusion, s32[23592]{0:T(1024)S(1)} %add_select_fusion.1, pred[23592]{0:T(1024)(128)(4,1)S(1)} %get-tuple-element.138), kind=kLoop, calls=%fused_computation.24 | loop fusion | flops 12055512 | bytes 12291432 | tf_op jit(solution)/shard_map/reduce_sum | solution.py:41
  257.6 2.5 collective-permute-start
  260.1 1.5 collective-permute-start.1
  261.6 115.3 %all-reduce.2.cloned.1.call-done = f32[23592]{0:T(1024)} async-done(((f32[23592]{0:T(1024)}), f32[23592]{0:T(1024)}) %all-reduce.2.cloned.1.call-update) | async-done | bytes 94384 | tf_op jit(solution)/shard_map/psum | solution.py:123
  376.9 1.5 broadcast_multiply_fusion
  378.5 1.2 fusion.77
  379.7 0.8 fusion.76
  380.7 0.8 fusion.92
  382.0 1.3 fusion.93
  383.4 0.3 stack.127
  383.8 1.2 gather_fusion.1
  385.0 0.3 select_reduce_fusion.1
  385.3 41.1 %psum.15 = f32[476]{0:T(512)S(1)} all-reduce(f32[476]{0:T(512)S(1)} %select_reduce_fusion.1), channel_id=1, replica_groups=mesh['dp'=4,'seq'=8] {'dp','seq'}, use_global_device_ids=true, to_apply=%region_38.39 | all-reduce | flops 476 | bytes 3808 | tf_op jit(solution)/shard_map/psum | solution.py:123
  426.4 0.6 broadcast_multiply_fusion.1
  427.2 4.5 %fusion.62 = bf16[2,64,1536]{2,1,0:T(8,128)(2,1)} fusion(bf16[2,64,1536]{2,1,0:T(8,128)(2,1)S(1)} %fusion.29, bf16[2,15,1536]{2,1,0:T(8,128)(2,1)S(1)} %collective-permute-done.1, bf16[2,15,1536]{2,1,0:T(8,128)(2,1)S(1)} %collective-permute-done, f32[1536]{0:T(1024)S(1)} %get-tuple-element.94, f32[1536]{0:T(1024)S(1)} %get-tuple-element.95, ...), kind=kLoop, calls=%fused_computation.155 | loop fusion | flops 35979264 | bytes 1161216 | tf_op jit(solution)/shard_map/convert_element_type | solution.py:105
  (194 shorter events, 0.8 us)
Async XLA Ops:
  7.2 10.8 %copy-start.7 = (bf16[31,1536]{1,0:T(8,128)(2,1)S(1)}, bf16[31,1536]{1,0:T(8,128)(2,1)}, u32[]{:S(2)}) copy-start(bf16[31,1536]{1,0:T(8,128)(2,1)} %param.18) | copy-start | bytes 285700
  7.2 12.4 %copy-start.69 = (s32[476]{0:T(512)S(1)}, s32[476]{0:T(512)}, u32[]{:S(2)}) copy-start(s32[476]{0:T(512)} %param.21) | copy-start | bytes 5716
  7.2 13.5 %copy-start.6 = (s32[23592]{0:T(1024)S(1)}, s32[23592]{0:T(1024)}, u32[]{:S(2)}) copy-start(s32[23592]{0:T(1024)} %param.20) | copy-start | bytes 283108
  7.2 66.1 %all-gather.5.cloned.1.call-start = ((), (), s32[]{:S(2)}) async-start(), calls=%async_computation.1 | async-start | bytes 3538944 | tf_op jit(solution)/shard_map/all_gather | solution.py:65
  9.5 125.2 %all-gather.3.cloned.1.call-start = ((), (), s32[]{:S(2)}) async-start(), calls=%async_computation | async-start | bytes 3538944 | tf_op jit(solution)/shard_map/all_gather | solution.py:66
  11.7 365.2 %all-reduce.2.cloned.1.call-start = ((), (), s32[]{:S(2)}) async-start(), calls=%async_computation.2 | async-start | bytes 196608 | tf_op jit(solution)/shard_map/psum | solution.py:123
  11.8 10.3 %collective-permute-start.2 = (bf16[2,15,1536]{2,1,0:T(8,128)(2,1)S(1)}, bf16[2,15,1536]{2,1,0:T(8,128)(2,1)S(1)}, u32[]{:S(2)}, u32[]{:S(2)}) collective-permute-start(bf16[2,15,1536]{2,1,0:T(8,128)(2,1)S(1)} %get-tuple-element.144), channel_id=1, source_target_pairs={{0,1},{1,2},{2,3},{3,4},{4,5},{5,6},{6,7},{8,9},{9,10},{10,11},{11... | collective-permute-start | bytes 276488 | tf_op jit(solution)/shard_map/ppermute | solution.py:21
  16.7 6.5 %collective-permute-start.3 = (bf16[2,15,1536]{2,1,0:T(8,128)(2,1)S(1)}, bf16[2,15,1536]{2,1,0:T(8,128)(2,1)S(1)}, u32[]{:S(2)}, u32[]{:S(2)}) collective-permute-start(bf16[2,15,1536]{2,1,0:T(8,128)(2,1)S(1)} %get-tuple-element.145), channel_id=1, source_target_pairs={{1,0},{2,1},{3,2},{4,3},{5,4},{6,5},{7,6},{9,8},{10,9},{11,10},{12... | collective-permute-start | bytes 276488 | tf_op jit(solution)/shard_map/ppermute | solution.py:22
  18.2 8.3 %copy-start.40 = (f32[1536]{0:T(1024)}, f32[1536]{0:T(1024)S(1)}, u32[]{:S(2)}) copy-start(f32[1536]{0:T(1024)S(1)} %get-tuple-element.112) | copy-start | bytes 18436
  18.3 8.3 %copy-start.42 = (f32[1536]{0:T(1024)}, f32[1536]{0:T(1024)S(1)}, u32[]{:S(2)}) copy-start(f32[1536]{0:T(1024)S(1)} %get-tuple-element.113) | copy-start | bytes 18436
  18.3 8.3 %copy-start.44 = (f32[1536]{0:T(1024)}, f32[1536]{0:T(1024)S(1)}, u32[]{:S(2)}) copy-start(f32[1536]{0:T(1024)S(1)} %get-tuple-element.114) | copy-start | bytes 18436
  18.3 8.3 %copy-start.46 = (f32[1536]{0:T(1024)}, f32[1536]{0:T(1024)S(1)}, u32[]{:S(2)}) copy-start(f32[1536]{0:T(1024)S(1)} %get-tuple-element.115) | copy-start | bytes 18436
  18.3 8.3 %copy-start.48 = (f32[1536]{0:T(1024)}, f32[1536]{0:T(1024)S(1)}, u32[]{:S(2)}) copy-start(f32[1536]{0:T(1024)S(1)} %get-tuple-element.116) | copy-start | bytes 18436
  18.3 8.3 %copy-start.50 = (f32[1536]{0:T(1024)}, f32[1536]{0:T(1024)S(1)}, u32[]{:S(2)}) copy-start(f32[1536]{0:T(1024)S(1)} %get-tuple-element.117) | copy-start | bytes 18436
  18.3 8.3 %copy-start.52 = (f32[1536]{0:T(1024)}, f32[1536]{0:T(1024)S(1)}, u32[]{:S(2)}) copy-start(f32[1536]{0:T(1024)S(1)} %get-tuple-element.118) | copy-start | bytes 18436
  18.3 8.3 %copy-start.54 = (f32[1536]{0:T(1024)}, f32[1536]{0:T(1024)S(1)}, u32[]{:S(2)}) copy-start(f32[1536]{0:T(1024)S(1)} %get-tuple-element.119) | copy-start | bytes 18436
  18.3 8.3 %copy-start.56 = (f32[1536]{0:T(1024)}, f32[1536]{0:T(1024)S(1)}, u32[]{:S(2)}) copy-start(f32[1536]{0:T(1024)S(1)} %get-tuple-element.120) | copy-start | bytes 18436
  18.3 8.3 %copy-start.58 = (f32[1536]{0:T(1024)}, f32[1536]{0:T(1024)S(1)}, u32[]{:S(2)}) copy-start(f32[1536]{0:T(1024)S(1)} %get-tuple-element.121) | copy-start | bytes 18436
  18.3 8.3 %copy-start.60 = (f32[1536]{0:T(1024)}, f32[1536]{0:T(1024)S(1)}, u32[]{:S(2)}) copy-start(f32[1536]{0:T(1024)S(1)} %get-tuple-element.122) | copy-start | bytes 18436
  18.4 8.3 %copy-start.62 = (f32[1536]{0:T(1024)}, f32[1536]{0:T(1024)S(1)}, u32[]{:S(2)}) copy-start(f32[1536]{0:T(1024)S(1)} %get-tuple-element.123) | copy-start | bytes 18436
  18.7 7.9 %copy-start.8 = (f32[1536]{0:T(1024)}, f32[1536]{0:T(1024)S(1)}, u32[]{:S(2)}) copy-start(f32[1536]{0:T(1024)S(1)} %get-tuple-element.96) | copy-start | bytes 18436
  18.7 7.9 %copy-start.10 = (f32[1536]{0:T(1024)}, f32[1536]{0:T(1024)S(1)}, u32[]{:S(2)}) copy-start(f32[1536]{0:T(1024)S(1)} %get-tuple-element.97) | copy-start | bytes 18436
  18.7 7.9 %copy-start.12 = (f32[1536]{0:T(1024)}, f32[1536]{0:T(1024)S(1)}, u32[]{:S(2)}) copy-start(f32[1536]{0:T(1024)S(1)} %get-tuple-element.98) | copy-start | bytes 18436
  18.7 7.9 %copy-start.14 = (f32[1536]{0:T(1024)}, f32[1536]{0:T(1024)S(1)}, u32[]{:S(2)}) copy-start(f32[1536]{0:T(1024)S(1)} %get-tuple-element.99) | copy-start | bytes 18436
  18.7 7.9 %copy-start.16 = (f32[1536]{0:T(1024)}, f32[1536]{0:T(1024)S(1)}, u32[]{:S(2)}) copy-start(f32[1536]{0:T(1024)S(1)} %get-tuple-element.100) | copy-start | bytes 18436
  18.7 7.9 %copy-start.18 = (f32[1536]{0:T(1024)}, f32[1536]{0:T(1024)S(1)}, u32[]{:S(2)}) copy-start(f32[1536]{0:T(1024)S(1)} %get-tuple-element.101) | copy-start | bytes 18436
  18.7 7.9 %copy-start.20 = (f32[1536]{0:T(1024)}, f32[1536]{0:T(1024)S(1)}, u32[]{:S(2)}) copy-start(f32[1536]{0:T(1024)S(1)} %get-tuple-element.102) | copy-start | bytes 18436
  18.8 7.9 %copy-start.22 = (f32[1536]{0:T(1024)}, f32[1536]{0:T(1024)S(1)}, u32[]{:S(2)}) copy-start(f32[1536]{0:T(1024)S(1)} %get-tuple-element.103) | copy-start | bytes 18436
  18.8 7.9 %copy-start.24 = (f32[1536]{0:T(1024)}, f32[1536]{0:T(1024)S(1)}, u32[]{:S(2)}) copy-start(f32[1536]{0:T(1024)S(1)} %get-tuple-element.104) | copy-start | bytes 18436
  18.8 7.9 %copy-start.26 = (f32[1536]{0:T(1024)}, f32[1536]{0:T(1024)S(1)}, u32[]{:S(2)}) copy-start(f32[1536]{0:T(1024)S(1)} %get-tuple-element.105) | copy-start | bytes 18436
  18.8 7.9 %copy-start.28 = (f32[1536]{0:T(1024)}, f32[1536]{0:T(1024)S(1)}, u32[]{:S(2)}) copy-start(f32[1536]{0:T(1024)S(1)} %get-tuple-element.106) | copy-start | bytes 18436
  18.8 7.9 %copy-start.30 = (f32[1536]{0:T(1024)}, f32[1536]{0:T(1024)S(1)}, u32[]{:S(2)}) copy-start(f32[1536]{0:T(1024)S(1)} %get-tuple-element.107) | copy-start | bytes 18436
  176.2 10.6 %copy-start.4 = (s32[24576]{0:T(1024)S(1)}, s32[24576]{0:T(1024)}, u32[]{:S(2)}) copy-start(s32[24576]{0:T(1024)} %pad_clamp_fusion) | copy-start | bytes 294916
  234.7 143.8 %copy-start.1 = (bf16[2,64,1536]{2,1,0:T(8,128)(2,1)S(1)}, bf16[2,64,1536]{2,1,0:T(8,128)(2,1)}, u32[]{:S(2)}) copy-start(bf16[2,64,1536]{2,1,0:T(8,128)(2,1)} %param.19) | copy-start | bytes 1179652
  257.6 120.9 %collective-permute-start = (bf16[2,15,1536]{2,1,0:T(8,128)(2,1)S(1)}, bf16[2,15,1536]{2,1,0:T(8,128)(2,1)S(1)}, u32[]{:S(2)}, u32[]{:S(2)}) collective-permute-start(bf16[2,15,1536]{2,1,0:T(8,128)(2,1)S(1)} %get-tuple-element.146), channel_id=1, source_target_pairs={{0,1},{1,2},{2,3},{3,4},{4,5},{5,6},{6,7},{8,9},{9,10},{10,11},{11... | collective-permute-start | bytes 276488 | tf_op jit(solution)/shard_map/ppermute | solution.py:21
  260.1 120.6 %collective-permute-start.1 = (bf16[2,15,1536]{2,1,0:T(8,128)(2,1)S(1)}, bf16[2,15,1536]{2,1,0:T(8,128)(2,1)S(1)}, u32[]{:S(2)}, u32[]{:S(2)}) collective-permute-start(bf16[2,15,1536]{2,1,0:T(8,128)(2,1)S(1)} %get-tuple-element.147), channel_id=1, source_target_pairs={{1,0},{2,1},{3,2},{4,3},{5,4},{6,5},{7,6},{9,8},{10,9},{11,10},{12... | collective-permute-start | bytes 276488 | tf_op jit(solution)/shard_map/ppermute | solution.py:22
  381.7 45.3 %copy-start.9 = (f32[1536]{0:T(1024)S(1)}, f32[1536]{0:T(1024)}, u32[]{:S(2)}) copy-start(f32[1536]{0:T(1024)} %copy-done.8) | copy-start | bytes 18436
  381.7 45.3 %copy-start.11 = (f32[1536]{0:T(1024)S(1)}, f32[1536]{0:T(1024)}, u32[]{:S(2)}) copy-start(f32[1536]{0:T(1024)} %copy-done.10) | copy-start | bytes 18436
  381.7 45.3 %copy-start.13 = (f32[1536]{0:T(1024)S(1)}, f32[1536]{0:T(1024)}, u32[]{:S(2)}) copy-start(f32[1536]{0:T(1024)} %copy-done.12) | copy-start | bytes 18436
  381.7 45.3 %copy-start.15 = (f32[1536]{0:T(1024)S(1)}, f32[1536]{0:T(1024)}, u32[]{:S(2)}) copy-start(f32[1536]{0:T(1024)} %copy-done.14) | copy-start | bytes 18436
  381.7 45.3 %copy-start.17 = (f32[1536]{0:T(1024)S(1)}, f32[1536]{0:T(1024)}, u32[]{:S(2)}) copy-start(f32[1536]{0:T(1024)} %copy-done.16) | copy-start | bytes 18436
  381.7 45.3 %copy-start.19 = (f32[1536]{0:T(1024)S(1)}, f32[1536]{0:T(1024)}, u32[]{:S(2)}) copy-start(f32[1536]{0:T(1024)} %copy-done.18) | copy-start | bytes 18436
  381.7 45.3 %copy-start.21 = (f32[1536]{0:T(1024)S(1)}, f32[1536]{0:T(1024)}, u32[]{:S(2)}) copy-start(f32[1536]{0:T(1024)} %copy-done.20) | copy-start | bytes 18436
  381.8 45.3 %copy-start.23 = (f32[1536]{0:T(1024)S(1)}, f32[1536]{0:T(1024)}, u32[]{:S(2)}) copy-start(f32[1536]{0:T(1024)} %copy-done.22) | copy-start | bytes 18436
  381.8 45.3 %copy-start.25 = (f32[1536]{0:T(1024)S(1)}, f32[1536]{0:T(1024)}, u32[]{:S(2)}) copy-start(f32[1536]{0:T(1024)} %copy-done.24) | copy-start | bytes 18436
  381.8 45.3 %copy-start.27 = (f32[1536]{0:T(1024)S(1)}, f32[1536]{0:T(1024)}, u32[]{:S(2)}) copy-start(f32[1536]{0:T(1024)} %copy-done.26) | copy-start | bytes 18436
  381.8 45.3 %copy-start.29 = (f32[1536]{0:T(1024)S(1)}, f32[1536]{0:T(1024)}, u32[]{:S(2)}) copy-start(f32[1536]{0:T(1024)} %copy-done.28) | copy-start | bytes 18436
  381.8 45.3 %copy-start.31 = (f32[1536]{0:T(1024)S(1)}, f32[1536]{0:T(1024)}, u32[]{:S(2)}) copy-start(f32[1536]{0:T(1024)} %copy-done.30) | copy-start | bytes 18436
  381.8 45.3 %copy-start.33 = (f32[1536]{0:T(1024)S(1)}, f32[1536]{0:T(1024)}, u32[]{:S(2)}) copy-start(f32[1536]{0:T(1024)} %copy-done.32) | copy-start | bytes 18436
  381.8 45.3 %copy-start.35 = (f32[1536]{0:T(1024)S(1)}, f32[1536]{0:T(1024)}, u32[]{:S(2)}) copy-start(f32[1536]{0:T(1024)} %copy-done.34) | copy-start | bytes 18436
  381.8 45.3 %copy-start.37 = (f32[1536]{0:T(1024)S(1)}, f32[1536]{0:T(1024)}, u32[]{:S(2)}) copy-start(f32[1536]{0:T(1024)} %copy-done.36) | copy-start | bytes 18436
  381.8 45.3 %copy-start.39 = (f32[1536]{0:T(1024)S(1)}, f32[1536]{0:T(1024)}, u32[]{:S(2)}) copy-start(f32[1536]{0:T(1024)} %copy-done.38) | copy-start | bytes 18436
  381.8 45.3 %copy-start.41 = (f32[1536]{0:T(1024)S(1)}, f32[1536]{0:T(1024)}, u32[]{:S(2)}) copy-start(f32[1536]{0:T(1024)} %copy-done.40) | copy-start | bytes 18436
  381.9 45.3 %copy-start.43 = (f32[1536]{0:T(1024)S(1)}, f32[1536]{0:T(1024)}, u32[]{:S(2)}) copy-start(f32[1536]{0:T(1024)} %copy-done.42) | copy-start | bytes 18436
  381.9 45.3 %copy-start.45 = (f32[1536]{0:T(1024)S(1)}, f32[1536]{0:T(1024)}, u32[]{:S(2)}) copy-start(f32[1536]{0:T(1024)} %copy-done.44) | copy-start | bytes 18436
  381.9 45.3 %copy-start.47 = (f32[1536]{0:T(1024)S(1)}, f32[1536]{0:T(1024)}, u32[]{:S(2)}) copy-start(f32[1536]{0:T(1024)} %copy-done.46) | copy-start | bytes 18436
  381.9 45.3 %copy-start.49 = (f32[1536]{0:T(1024)S(1)}, f32[1536]{0:T(1024)}, u32[]{:S(2)}) copy-start(f32[1536]{0:T(1024)} %copy-done.48) | copy-start | bytes 18436
  381.9 45.3 %copy-start.51 = (f32[1536]{0:T(1024)S(1)}, f32[1536]{0:T(1024)}, u32[]{:S(2)}) copy-start(f32[1536]{0:T(1024)} %copy-done.50) | copy-start | bytes 18436
  381.9 45.3 %copy-start.53 = (f32[1536]{0:T(1024)S(1)}, f32[1536]{0:T(1024)}, u32[]{:S(2)}) copy-start(f32[1536]{0:T(1024)} %copy-done.52) | copy-start | bytes 18436
  381.9 45.3 %copy-start.55 = (f32[1536]{0:T(1024)S(1)}, f32[1536]{0:T(1024)}, u32[]{:S(2)}) copy-start(f32[1536]{0:T(1024)} %copy-done.54) | copy-start | bytes 18436
  381.9 45.3 %copy-start.57 = (f32[1536]{0:T(1024)S(1)}, f32[1536]{0:T(1024)}, u32[]{:S(2)}) copy-start(f32[1536]{0:T(1024)} %copy-done.56) | copy-start | bytes 18436
  381.9 45.3 %copy-start.59 = (f32[1536]{0:T(1024)S(1)}, f32[1536]{0:T(1024)}, u32[]{:S(2)}) copy-start(f32[1536]{0:T(1024)} %copy-done.58) | copy-start | bytes 18436
  381.9 45.3 %copy-start.61 = (f32[1536]{0:T(1024)S(1)}, f32[1536]{0:T(1024)}, u32[]{:S(2)}) copy-start(f32[1536]{0:T(1024)} %copy-done.60) | copy-start | bytes 18436
  382.0 45.3 %copy-start.63 = (f32[1536]{0:T(1024)S(1)}, f32[1536]{0:T(1024)}, u32[]{:S(2)}) copy-start(f32[1536]{0:T(1024)} %copy-done.62) | copy-start | bytes 18436
  (17 other events, 85.8 us)
Sparse Core Ops, SparseCore 0:
  10.2 63.0 all-gather.4
  75.5 59.0 all-gather.2
  257.7 119.1 all-reduce.1
where the time goes:
time: 440 us; the launch traced here: 438 us
  waiting for transfers between devices  214 us (49%)
  local copies, waits for them, and re-layouts  98.6 us (22%)
  other arithmetic  44.2 us (10%)
  blocking collectives  41.1 us (9%)
  between operations  15.2 us (3%)
  matrix products  14.8 us (3%)
  starting transfers between devices  10.2 us (2%)
    psum x1, waiting for transfers between devices, on_device(): weight_sum, kernel_sum = lax.psum((weight_vals, kernel_vals), ('dp', 'seq'))  115 us
    all_gather x1, waiting for transfers between devices, on_device(): lax.all_gather(value_rows, 'seq', axis=1, tiled=True)  54.3 us
    gather x2, local copies, waits for them, and re-layouts, pick_entries(): chosen = jnp.take(blocks, picks // lane, axis=0)  49.1 us
    all_gather x1, waiting for transfers between devices, on_device(): lax.all_gather(key_rows, 'seq', axis=1, tiled=True)  43.4 us
    psum x1, blocking collectives, on_device(): weight_sum, kernel_sum = lax.psum((weight_vals, kernel_vals), ('dp', 'seq'))  41.1 us
    reduce_sum x2, other arithmetic, pick_entries(): return jnp.sum(jnp.where(hit, chosen, jnp.float32(0.0)), axis=1)  23.2 us
    unnamed x148, local copies, waits for them, and re-layouts  21.1 us
    another operation x2, local copies, waits for them, and re-layouts, pick_entries(): blocks = flat.reshape(flat.shape[0] // lane, lane)  10.6 us
  transfers between devices with their start and end apart: 7, of which 4 were waited for; matrix products, arithmetic and copies ran while one was open for 5% of the time, Pallas kernels for 0%

commit v1 on v0

--- a/solution.py
+++ b/solution.py
@@ -1,8 +1,11 @@
+import functools
 import math
 
 import jax
 import jax.numpy as jnp
 from jax import lax
+from jax.experimental import pallas as pl
+from jax.experimental.pallas import tpu as pltpu
 from jax.sharding import PartitionSpec as P
 
 HEADS = 16
@@ -39,6 +42,272 @@
     lane_ids = jnp.arange(lane, dtype=jnp.int32)
     hit = lane_ids[None, :] == (picks % lane)[:, None]
     return jnp.sum(jnp.where(hit, chosen, jnp.float32(0.0)), axis=1)
+
+
+def peers_of(axis, count):
+    me = lax.axis_index(axis)
+    return [lax.rem(me + step, count) for step in range(1, count)]
+
+
+def greet(axes):
+    barrier = pltpu.get_barrier_semaphore()
+    total = 0
+    for axis, count in axes:
+        for peer in peers_of(axis, count):
+            pl.semaphore_signal(
+                barrier, inc=1, device_id={axis: peer}, device_id_type=pl.DeviceIdType.MESH
+            )
+            total += 1
+    pl.semaphore_wait(barrier, total)
+
+
+def send_to(src, dst, send_sem, recv_sem, axis, peer):
+    copy = pltpu.make_async_remote_copy(
+        src_ref=src,
+        dst_ref=dst,
+        send_sem=send_sem,
+        recv_sem=recv_sem,
+        device_id={axis: peer},
+        device_id_type=pl.DeviceIdType.MESH,
+    )
+    copy.start()
+    return copy
+
+
+def attention_kernel(
+    count,
+    score_scale,
+    len_ref,
+    q_ref,
+    k_ref,
+    v_ref,
+    out_ref,
+    send,
+    recv,
+    back,
+    home,
+    send_sem,
+    recv_sem,
+    back_sem,
+    home_sem,
+):
+    utts, frames, width = q_ref.shape
+    block = width // count
+    head_size = width // HEADS
+    me = lax.axis_index("seq")
+    greet((("seq", count),))
+    for owner in range(count):
+        for utt in range(utts):
+            for place, ref in enumerate((q_ref, k_ref, v_ref)):
+                begin = (utt * 3 + place) * block
+                send[owner, :, begin : begin + block] = ref[
+                    utt, :, owner * block : (owner + 1) * block
+                ]
+    copies = [
+        send_to(send.at[peer], recv.at[me], send_sem.at[i], recv_sem.at[i], "seq", peer)
+        for i, peer in enumerate(peers_of("seq", count))
+    ]
+    recv[pl.ds(me, 1)] = send[pl.ds(me, 1)]
+    for copy in copies:
+        copy.wait_recv()
+    full = count * frames
+    ids = lax.broadcasted_iota(jnp.int32, (full, full), 1)
+    for utt in range(utts):
+        key_ok = ids < len_ref[utt]
+        for head in range(block // head_size):
+            parts = []
+            for place in range(3):
+                begin = (utt * 3 + place) * block + head * head_size
+                parts.append(recv[:, :, begin : begin + head_size].reshape(full, head_size))
+            query, key, value = parts
+            scores = lax.dot_general(
+                query, key, (((1,), (1,)), ((), ())), preferred_element_type=jnp.float32
+            )
+            scores = jnp.where(key_ok, scores * score_scale, neg_big)
+            probs = jnp.exp(scores - jnp.max(scores, axis=-1, keepdims=True))
+            denom = jnp.sum(probs, axis=-1, keepdims=True)
+            rows = jnp.dot(probs.astype(jnp.bfloat16), value, preferred_element_type=jnp.float32)
+            rows = (rows / denom).astype(jnp.bfloat16)
+            begin = utt * block + head * head_size
+            back[:, :, begin : begin + head_size] = rows.reshape(count, frames, head_size)
+    returns = [
+        send_to(back.at[peer], home.at[me], back_sem.at[i], home_sem.at[i], "seq", peer)
+        for i, peer in enumerate(peers_of("seq", count))
+    ]
+    home[pl.ds(me, 1)] = back[pl.ds(me, 1)]
+    for copy in returns:
+        copy.wait_recv()
+    for owner in range(count):
+        for utt in range(utts):
+            out_ref[utt, :, owner * block : (owner + 1) * block] = home[
+                owner, :, utt * block : (utt + 1) * block
+            ]
+    for copy in copies + returns:
+        copy.wait_send()
+
+
+def exchanged_attention(queries, key_rows, value_rows, utt_lengths, score_scale):
+    utts, frames, width = queries.shape
+    count = lax.axis_size("seq")
+    block = width // count
+    vmem = pl.BlockSpec(memory_space=pltpu.VMEM)
+    wide = pltpu.VMEM((count, frames, 3 * utts * block), jnp.bfloat16)
+    narrow = pltpu.VMEM((count, frames, utts * block), jnp.bfloat16)
+    sems = pltpu.SemaphoreType.DMA((count - 1,))
+    return pl.pallas_call(
+        functools.partial(attention_kernel, count, score_scale),
+        out_shape=jax.ShapeDtypeStruct(queries.shape, jnp.bfloat16),
+        in_specs=[pl.BlockSpec(memory_space=pltpu.SMEM), vmem, vmem, vmem],
+        out_specs=vmem,
+        scratch_shapes=[wide, wide, narrow, narrow, sems, sems, sems, sems],
+        compiler_params=pltpu.CompilerParams(
+            collective_id=0, has_side_effects=True, vmem_limit_bytes=40 * 2**20
+        ),
+    )(utt_lengths, queries, key_rows, value_rows)
+
+
+def total_kernel(
+    n_seq, n_dp, x_ref, out_ref, parts, mine, sums, whole, s1, r1, s2, r2, s3, r3
+):
+    me = lax.axis_index("seq")
+    me_dp = lax.axis_index("dp")
+    greet((("seq", n_seq), ("dp", n_dp)))
+    copies = [
+        send_to(x_ref.at[peer], parts.at[me], s1.at[i], r1.at[i], "seq", peer)
+        for i, peer in enumerate(peers_of("seq", n_seq))
+    ]
+    parts[pl.ds(me, 1)] = x_ref[pl.ds(me, 1)]
+    for copy in copies:
+        copy.wait_recv()
+    mine[...] = jnp.sum(parts[...], axis=0)
+    second = [
+        send_to(mine, sums.at[me_dp], s2.at[i], r2.at[i], "dp", peer)
+        for i, peer in enumerate(peers_of("dp", n_dp))
+    ]
+    sums[pl.ds(me_dp, 1)] = mine[...][None]
+    for copy in second:
+        copy.wait_recv()
+    whole[pl.ds(me, 1)] = jnp.sum(sums[...], axis=0)[None]
+    third = [
+        send_to(whole.at[me], whole.at[me], s3.at[i], r3.at[i], "seq", peer)
+        for i, peer in enumerate(peers_of("seq", n_seq))
+    ]
+    for copy in third:
+        copy.wait_recv()
+    out_ref[...] = whole[...]
+    for copy in copies + second + third:
+        copy.wait_send()
+
+
+def summed(values):
+    n_seq, n_dp = lax.axis_size("seq"), lax.axis_size("dp")
+    chunk = 128 * 8 * n_seq
+    rows = -(-values.shape[0] // chunk) * 8
+    x = jnp.pad(values, (0, rows * 128 * n_seq - values.shape[0])).reshape(n_seq, rows, 128)
+    vmem = pl.BlockSpec(memory_space=pltpu.VMEM)
+    seq_sems = pltpu.SemaphoreType.DMA((n_seq - 1,))
+    dp_sems = pltpu.SemaphoreType.DMA((n_dp - 1,))
+    out = pl.pallas_call(
+        functools.partial(total_kernel, n_seq, n_dp),
+        out_shape=jax.ShapeDtypeStruct(x.shape, jnp.float32),
+        in_specs=[vmem],
+        out_specs=vmem,
+        scratch_shapes=[
+            pltpu.VMEM(x.shape, jnp.float32),
+            pltpu.VMEM((rows, 128), jnp.float32),
+            pltpu.VMEM((n_dp, rows, 128), jnp.float32),
+            pltpu.VMEM(x.shape, jnp.float32),
+            seq_sems,
+            seq_sems,
+            dp_sems,
+            dp_sems,
+            seq_sems,
+            seq_sems,
+        ],
+        compiler_params=pltpu.CompilerParams(collective_id=1, has_side_effects=True),
+    )(x)
+    return out.reshape(-1)
+
+
+LOW = 256
+PICK_TILE = 512
+
+
+def choose(stacked, tokens, index):
+    low = lax.rem(index, LOW)
+    high = lax.div(index, LOW)
+    hot = lax.broadcasted_iota(jnp.int32, (LOW, index.shape[1]), 0) == low
+    hot = jnp.where(hot, 1.0, 0.0).astype(jnp.bfloat16)
+    every = jnp.dot(stacked, hot, preferred_element_type=jnp.float32)
+    out = every[:tokens]
+    for part in range(1, stacked.shape[0] // tokens):
+        out = jnp.where(high == part, every[part * tokens : (part + 1) * tokens], out)
+    return out
+
+
+def picks_kernel(pick_ref, ctx_ref, grad_ref, out_ref, ctx_stack, grad_stack):
+    tokens, width = ctx_ref.shape
+
+    @pl.when(pl.program_id(0) == 0)
+    def _():
+        for part in range(width // LOW):
+            cols = slice(part * LOW, (part + 1) * LOW)
+            rows = slice(part * tokens, (part + 1) * tokens)
+            ctx_stack[rows, :] = ctx_ref[:, cols]
+            grad_stack[rows, :] = grad_ref[:, cols]
+
+    pick = pick_ref[...]
+    left = choose(ctx_stack[...], tokens, lax.div(pick, width))
+    right = choose(grad_stack[...], tokens, lax.rem(pick, width))
+    out_ref[...] = jnp.sum(left * right, axis=0, keepdims=True)
+
+
+def picked_products(ctx, grad, picks):
+    tokens, width = ctx.shape
+    steps = -(-picks.shape[0] // PICK_TILE)
+    padded_picks = jnp.pad(picks, (0, steps * PICK_TILE - picks.shape[0])).reshape(1, -1)
+    whole = pl.BlockSpec((tokens, width), lambda i: (0, 0))
+    tile = pl.BlockSpec((1, PICK_TILE), lambda i: (0, i))
+    stack = pltpu.VMEM((tokens * width // LOW, LOW), jnp.bfloat16)
+    out = pl.pallas_call(
+        picks_kernel,
+        grid=(steps,),
+        out_shape=jax.ShapeDtypeStruct(padded_picks.shape, jnp.float32),
+        in_specs=[tile, whole, whole],
+        out_specs=tile,
+        scratch_shapes=[stack, stack],
+        compiler_params=pltpu.CompilerParams(vmem_limit_bytes=40 * 2**20),
+    )(padded_picks, ctx, grad)
+    return out.reshape(-1)
+
+
+def gathered_attention(queries, key_rows, value_rows, utt_lengths, score_scale):
+    local_utts, frames_dev, width = queries.shape
+    full_frames = frames_dev * lax.axis_size("seq")
+    head_size = width // HEADS
+    all_keys, all_values = (
+        lax.all_gather(key_rows, "seq", axis=1, tiled=True),
+        lax.all_gather(value_rows, "seq", axis=1, tiled=True),
+    )
+    full_ids = jnp.arange(full_frames, dtype=jnp.int32)
+
+    def one_utt(item):
+        query_utt, key_utt, value_utt, length_utt = item
+        query_heads = query_utt.reshape(frames_dev, HEADS, head_size)
+        key_heads = key_utt.reshape(full_frames, HEADS, head_size)
+        value_heads = value_utt.reshape(full_frames, HEADS, head_size)
+        scores = (
+            jnp.einsum("qhd,khd->hqk", query_heads, key_heads, preferred_element_type=jnp.float32)
+            * score_scale
+        )
+        weights, denom = softmax_rows(scores, (full_ids < length_utt)[None, None, :])
+        out_rows = jnp.einsum(
+            "hqk,khd->qhd", weights, value_heads, preferred_element_type=jnp.float32
+        )
+        out_rows = out_rows / denom.transpose(1, 0)[:, :, None]
+        return out_rows.astype(jnp.bfloat16).reshape(frames_dev, width)
+
+    return lax.map(one_utt, (queries, all_keys, all_values, utt_lengths))
 
 
 def on_device(
@@ -61,29 +330,10 @@
     first_frame = lax.axis_index("seq") * frames_dev
     local_ids = first_frame + jnp.arange(frames_dev, dtype=jnp.int32)
     valid_rows = (local_ids[None, :] < utt_lengths[:, None]).astype(jnp.float32)
-    all_keys, all_values = (
-        lax.all_gather(key_rows, "seq", axis=1, tiled=True),
-        lax.all_gather(value_rows, "seq", axis=1, tiled=True),
-    )
-    full_ids = jnp.arange(full_frames, dtype=jnp.int32)
-
-    def one_utt(item):
-        query_utt, key_utt, value_utt, length_utt = item
-        query_heads = query_utt.reshape(frames_dev, HEADS, head_size)
-        key_heads = key_utt.reshape(full_frames, HEADS, head_size)
-        value_heads = value_utt.reshape(full_frames, HEADS, head_size)
-        scores = (
-            jnp.einsum("qhd,khd->hqk", query_heads, key_heads, preferred_element_type=jnp.float32)
-            * score_scale
-        )
-        weights, denom = softmax_rows(scores, (full_ids < length_utt)[None, None, :])
-        out_rows = jnp.einsum(
-            "hqk,khd->qhd", weights, value_heads, preferred_element_type=jnp.float32
-        )
-        out_rows = out_rows / denom.transpose(1, 0)[:, :, None]
-        return out_rows.astype(jnp.bfloat16).reshape(frames_dev, width)
-
-    context = lax.map(one_utt, (queries, all_keys, all_values, utt_lengths))
+    if HEADS % seq_count == 0:
+        context = exchanged_attention(queries, key_rows, value_rows, utt_lengths, score_scale)
+    else:
+        context = gathered_attention(queries, key_rows, value_rows, utt_lengths, score_scale)
     context_flat = context.reshape(local_utts * frames_dev, width)
     projected = jnp.dot(context_flat, out_weight, preferred_element_type=jnp.float32).reshape(
         local_utts, frames_dev, width
@@ -111,16 +361,15 @@
         back_sum = back_sum + kernel_f[offset] * cot_pad[:, begin : begin + frames_dev]
     hidden_grad = (back_sum * valid_rows[:, :, None]).astype(jnp.bfloat16)
     grad_flat = hidden_grad.reshape(local_utts * frames_dev, width)
-    weight_grad = lax.dot_general(
-        context_flat, grad_flat, (((0,), (0,)), ((), ())), preferred_element_type=jnp.float32
-    )
     context_grad = lax.dot_general(
         grad_flat, out_weight, (((1,), (1,)), ((), ())), preferred_element_type=jnp.float32
     )
     context_grad = context_grad.reshape(local_utts, frames_dev, width).astype(jnp.bfloat16)
-    weight_vals = pick_entries(weight_grad, pick_weight)
+    weight_vals = picked_products(context_flat, grad_flat, pick_weight)
     kernel_vals = pick_entries(kernel_grad, pick_kernel)
-    weight_sum, kernel_sum = lax.psum((weight_vals, kernel_vals), ("dp", "seq"))
+    total = summed(jnp.concatenate([weight_vals, kernel_vals]))
+    weight_sum = total[: pick_weight.shape[0]]
+    kernel_sum = total[weight_vals.shape[0] : weight_vals.shape[0] + pick_kernel.shape[0]]
     total_slots = local_utts * lax.axis_size("dp") * full_frames
     norm_factor = 1.0 / math.sqrt(total_slots)
     return (conv_out, context_grad, weight_sum * norm_factor, kernel_sum * norm_factor)

time: 440 us -> 141 us (0.32)
  waiting for transfers between devices: 214 us -> 4.32 us
  Pallas kernels: 0 us -> 93 us
  local copies, waits for them, and re-layouts: 98.6 us -> 7.03 us
  blocking collectives: 41.1 us -> 0 us
  other arithmetic: 44.2 us -> 16.6 us
  between operations: 15.2 us -> 1.19 us
  matrix products: 14.8 us -> 7.89 us
    psum x1 -> x0, waiting for transfers between devices: 115 us -> none  [on_device(): weight_sum, kernel_sum = lax.psum((weight_vals, kernel_vals), ('dp', 'seq'))]
    all_gather x2 -> x0, waiting for transfers between devices: 97.7 us -> none  [the longest x1 54.3 us: on_device(): lax.all_gather(value_rows, 'seq', axis=1, tiled=True)]
    pallas_call x0 -> x3, Pallas kernels: none -> 93 us  [the longest x1 46.1 us: exchanged_attention(): pl.pallas_call(functools.partial(attention_kernel, count, score_scale), o...]
    gather x2 -> x1, local copies, waits for them, and re-layouts: 49.1 us -> 1.19 us  [pick_entries(): chosen = jnp.take(blocks, picks // lane, axis=0)]
    psum x1 -> x0, blocking collectives: 41.1 us -> none  [on_device(): weight_sum, kernel_sum = lax.psum((weight_vals, kernel_vals), ('dp', 'seq'))]
    reduce_sum x2 -> x1, other arithmetic: 23.2 us -> 0.29 us  [pick_entries(): return jnp.sum(jnp.where(hit, chosen, jnp.float32(0.0)), axis=1)]
    unnamed x148 -> x18, local copies, waits for them, and re-layouts: 21.1 us -> 3.67 us
    another operation x2 -> x1, local copies, waits for them, and re-layouts: 10.6 us -> 0.02 us  [pick_entries(): blocks = flat.reshape(flat.shape[0] // lane, lane)]
  transfers between devices with their start and end apart: 7 -> 4, of which waited for: 4 -> 1; matrix products, arithmetic and copies ran while one was open for 5% -> 7% of each run, Pallas kernels for 0% -> 33%
where the time goes in v1:
time: 141 us
  Pallas kernels  93 us (66%)
  other arithmetic  16.6 us (12%)
  starting transfers between devices  10.7 us (8%)
  matrix products  7.89 us (6%)
  local copies, waits for them, and re-layouts  7.03 us (5%)
  waiting for transfers between devices  4.32 us (3%)
    pallas_call x1, Pallas kernels, exchanged_attention(): pl.pallas_call(functools.partial(attention_kernel, count, score_scale), o...  46.1 us
    pallas_call x1, Pallas kernels, picked_products(): pl.pallas_call(picks_kernel, grid=(steps,), out_shape=jax.ShapeDtypeStruc...  29.1 us
    pallas_call x1, Pallas kernels, summed(): pl.pallas_call(functools.partial(total_kernel, n_seq, n_dp), out_shape=ja...  17.8 us
    ppermute x2, starting transfers between devices, padded(): before = lax.ppermute(last, axis, up)  7.98 us
    dot_general x1, matrix products, on_device(): lax.dot_general(grad_flat, out_weight, (((1,), (1,)), ((), ())), preferre...  4.73 us
    convert_element_type x1, other arithmetic, on_device(): conv_out = conv_sum.astype(jnp.bfloat16)  4.43 us
    ppermute x2, waiting for transfers between devices, padded(): after = lax.ppermute(leading, axis, down)  4.32 us
    reduce_sum x4, other arithmetic, on_device(): kernel_rows.append(jnp.sum(window * cot_f, axis=(0, 1)))  4.18 us
  transfers between devices with their start and end apart: 4, of which 1 were waited for; matrix products, arithmetic and copies ran while one was open for 7% of the time, Pallas kernels for 33%

profile of v1, /device:TPU:0, one launch (start us, length us, event | category | flops | bytes accessed | tf_op | source)
XLA Modules:
  0.0 140.8 jit_solution(9583714964889545333)
XLA Ops:
  0.6 0.0 copy-start.5
  0.6 1.0 fusion.139
  1.7 4.8 %collective-permute-start.2 = (bf16[2,15,1536]{2,1,0:T(8,128)(2,1)S(1)}, bf16[2,15,1536]{2,1,0:T(8,128)(2,1)S(1)}, u32[]{:S(2)}, u32[]{:S(2)}) collective-permute-start(bf16[2,15,1536]{2,1,0:T(8,128)(2,1)S(1)} %get-tuple-element.68), channel_id=1, source_target_pairs={{0,1},{1,2},{2,3},{3,4},{4,5},{5,6},{6,7},{8,9},{9,10},{10,11},{11... | collective-permute-start | bytes 276488 | tf_op jit(solution)/shard_map/ppermute | solution.py:24
  6.5 1.3 collective-permute-start.3
  7.8 0.7 compare_convert_fusion
  8.6 0.0 copy-start
  8.6 1.0 copy-done
  9.6 0.0 copy-start.1
  9.6 1.0 copy-done.1
  10.6 0.0 copy-start.2
  10.6 1.0 copy-done.2
  11.6 0.0 copy-start.3
  11.6 0.7 copy-done.3
  12.2 46.1 %shard_map.129 = bf16[2,64,1536]{2,1,0:T(8,128)(2,1)S(1)} custom-call(s32[2]{0:T(128)S(1)} %copy-done.3, bf16[2,64,1536]{2,1,0:T(8,128)(2,1)S(1)} %copy-done, bf16[2,64,1536]{2,1,0:T(8,128)(2,1)S(1)} %copy-done.1, bf16[2,64,1536]{2,1,0:T(8,128)(2,1)S(1)} %copy-done.2), custom_call_target="tpu_custom_call" | custom-call | tf_op jit(solution)/shard_map/pallas_call | solution.py:157
  58.3 0.0 copy-done.5
  58.4 0.0 copy-start.8
  58.4 0.0 copy-start.7
  58.4 3.2 %fusion.13 = bf16[2,64,1536]{2,1,0:T(8,128)(2,1)S(1)} fusion(bf16[2,64,1536]{2,1,0:T(8,128)(2,1)S(1)} %shard_map.129, bf16[1536,1536]{1,0:T(8,128)(2,1)} %param.15, bf16[2,64,1536]{2,1,0:T(8,128)(2,1)S(1)} %copy-done.5, f32[2,64]{1,0:T(2,128)S(1)} %compare_convert_fusion), kind=kOutput, calls=%fused_computation.39 | convolution fusion | flops 604766208 | bytes 5898752 | tf_op jit(solution)/shard_map/dot_general | solution.py:338
  61.5 0.0 copy-start.6
  61.6 0.0 copy-start.4
  61.6 3.1 %collective-permute-start = (bf16[2,15,1536]{2,1,0:T(8,128)(2,1)S(1)}, bf16[2,15,1536]{2,1,0:T(8,128)(2,1)S(1)}, u32[]{:S(2)}, u32[]{:S(2)}) collective-permute-start(bf16[2,15,1536]{2,1,0:T(8,128)(2,1)S(1)} %get-tuple-element.70), channel_id=1, source_target_pairs={{0,1},{1,2},{2,3},{3,4},{4,5},{5,6},{6,7},{8,9},{9,10},{10,11},{11... | collective-permute-start | bytes 276488 | tf_op jit(solution)/shard_map/ppermute | solution.py:24
  64.7 1.5 %collective-permute-start.1 = (bf16[2,15,1536]{2,1,0:T(8,128)(2,1)S(1)}, bf16[2,15,1536]{2,1,0:T(8,128)(2,1)S(1)}, u32[]{:S(2)}, u32[]{:S(2)}) collective-permute-start(bf16[2,15,1536]{2,1,0:T(8,128)(2,1)S(1)} %get-tuple-element.71), channel_id=1, source_target_pairs={{1,0},{2,1},{3,2},{4,3},{5,4},{6,5},{7,6},{9,8},{10,9},{11,10},{12... | collective-permute-start | bytes 276488 | tf_op jit(solution)/shard_map/ppermute | solution.py:25
  66.2 0.0 copy-done.8
  66.3 0.0 copy-done.7
  66.3 0.2 slice_reduce_fusion.29
  66.5 0.3 slice_reduce_fusion.30
  66.8 0.0 copy-done.6
  66.9 0.1 reshape.102.pick_ref
  66.9 4.3 %collective-permute-done.1 = bf16[2,15,1536]{2,1,0:T(8,128)(2,1)S(1)} collective-permute-done((bf16[2,15,1536]{2,1,0:T(8,128)(2,1)S(1)}, bf16[2,15,1536]{2,1,0:T(8,128)(2,1)S(1)}, u32[]{:S(2)}, u32[]{:S(2)}) %collective-permute-start.1) | collective-permute-done | bytes 92192 | tf_op jit(solution)/shard_map/ppermute | solution.py:25
  71.3 0.0 copy-done.4
  71.3 1.3 fusion.77
  72.6 0.9 fusion.76
  73.5 0.0 collective-permute-done
  73.5 1.2 fusion.61
  74.7 0.8 fusion.60
  75.9 0.3 stack.127
  76.3 1.2 gather_fusion
  77.5 0.0 collective-permute-done.2
  77.5 0.0 collective-permute-done.3
  77.5 0.2 maximum_convert_fusion
  77.7 3.1 %fusion.80 = bf16[2,64,1536]{2,1,0:T(8,128)(2,1)S(1)} fusion(f32[2,94,1536]{2,1,0:T(8,128)S(1)} %maximum_convert_fusion, f32[1536]{0:T(1024)S(1)} %get-tuple-element.36, f32[1536]{0:T(1024)S(1)} %get-tuple-element.37, f32[1536]{0:T(1024)S(1)} %get-tuple-element.38, f32[1536]{0:T(1024)S(1)} %get-tuple-element.39, f32[1536]{0:T(1024)S(1)} %get-tuple-element.40, ...), kind=kLoop, calls=%fused_computation.164 | loop fusion | flops 12386304 | bytes 24963584 | tf_op jit(solution)/shard_map/convert_element_type | solution.py:362
  80.8 29.1 %shard_map.130 = f32[1,24064]{1,0:T(1,128)S(1)} custom-call(s32[1,24064]{1,0:T(1,128)S(1)} %reshape.102.pick_ref, bf16[128,1536]{1,0:T(8,128)(2,1)S(1)} %bitcast.20, bf16[128,1536]{1,0:T(8,128)(2,1)S(1)} %bitcast.19), custom_call_target="tpu_custom_call" | custom-call | tf_op jit(solution)/shard_map/pallas_call | solution.py:272
  109.9 0.2 reduce.31
  110.1 0.3 select_reduce_fusion
  110.4 0.7 select_maximum_fusion
  111.1 17.8 %shard_map.131 = f32[8,24,128]{2,1,0:T(8,128)} custom-call(f32[8,24,128]{2,1,0:T(8,128)} %bitcast.23), custom_call_target="tpu_custom_call" | custom-call | tf_op jit(solution)/shard_map/pallas_call | solution.py:210
  128.9 1.3 slice_multiply_fusion.32
  130.1 1.5 %slice_multiply_fusion.31 = f32[23592]{0:T(1024)} fusion(f32[24576]{0:T(1024)} %bitcast.22), kind=kLoop, calls=%fused_computation.257 | loop fusion | flops 23592 | bytes 188736 | tf_op jit(solution)/shard_map/mul | solution.py:375
  131.6 4.7 %fusion.10 = bf16[2,64,1536]{2,1,0:T(8,128)(2,1)} fusion(bf16[2,64,1536]{2,1,0:T(8,128)(2,1)S(1)} %fusion.80, bf16[1536,1536]{1,0:T(8,128)(2,1)} %param.15), kind=kOutput, calls=%fused_computation.38 | convolution fusion | flops 604176384 | bytes 5505024 | tf_op jit(solution)/shard_map/dot_general | solution.py:364
  136.4 4.4 %fusion.46 = bf16[2,64,1536]{2,1,0:T(8,128)(2,1)} fusion(bf16[2,64,1536]{2,1,0:T(8,128)(2,1)S(1)} %fusion.13, bf16[2,15,1536]{2,1,0:T(8,128)(2,1)S(1)} %collective-permute-done.1, bf16[2,15,1536]{2,1,0:T(8,128)(2,1)S(1)} %collective-permute-done, f32[1536]{0:T(1024)S(1)} %get-tuple-element.36, f32[1536]{0:T(1024)S(1)} %get-tuple-element.37, ...), kind=kLoop, calls=%fused_computation.129 | loop fusion | flops 35979264 | bytes 1161216 | tf_op jit(solution)/shard_map/convert_element_type | solution.py:355
  (39 shorter events, 0.3 us)
Async XLA Ops:
  0.6 57.7 %copy-start.5 = (bf16[2,64,1536]{2,1,0:T(8,128)(2,1)S(1)}, bf16[2,64,1536]{2,1,0:T(8,128)(2,1)}, u32[]{:S(2)}) copy-start(bf16[2,64,1536]{2,1,0:T(8,128)(2,1)} %param.13) | copy-start | bytes 1179652
  1.7 75.8 %collective-permute-start.2 = (bf16[2,15,1536]{2,1,0:T(8,128)(2,1)S(1)}, bf16[2,15,1536]{2,1,0:T(8,128)(2,1)S(1)}, u32[]{:S(2)}, u32[]{:S(2)}) collective-permute-start(bf16[2,15,1536]{2,1,0:T(8,128)(2,1)S(1)} %get-tuple-element.68), channel_id=1, source_target_pairs={{0,1},{1,2},{2,3},{3,4},{4,5},{5,6},{6,7},{8,9},{9,10},{10,11},{11... | collective-permute-start | bytes 276488 | tf_op jit(solution)/shard_map/ppermute | solution.py:24
  6.5 71.0 %collective-permute-start.3 = (bf16[2,15,1536]{2,1,0:T(8,128)(2,1)S(1)}, bf16[2,15,1536]{2,1,0:T(8,128)(2,1)S(1)}, u32[]{:S(2)}, u32[]{:S(2)}) collective-permute-start(bf16[2,15,1536]{2,1,0:T(8,128)(2,1)S(1)} %get-tuple-element.69), channel_id=1, source_target_pairs={{1,0},{2,1},{3,2},{4,3},{5,4},{6,5},{7,6},{9,8},{10,9},{11,10},{12... | collective-permute-start | bytes 276488 | tf_op jit(solution)/shard_map/ppermute | solution.py:25
  8.6 1.0 copy-start
  9.6 1.0 copy-start.1
  10.6 1.0 copy-start.2
  11.6 0.7 copy-start.3
  58.4 7.9 %copy-start.8 = (s32[476]{0:T(512)S(1)}, s32[476]{0:T(512)}, u32[]{:S(2)}) copy-start(s32[476]{0:T(512)} %param.19) | copy-start | bytes 5716
  58.4 7.9 %copy-start.7 = (bf16[31,1536]{1,0:T(8,128)(2,1)S(1)}, bf16[31,1536]{1,0:T(8,128)(2,1)}, u32[]{:S(2)}) copy-start(bf16[31,1536]{1,0:T(8,128)(2,1)} %param.16) | copy-start | bytes 285700
  61.5 5.3 %copy-start.6 = (s32[23592]{0:T(1024)S(1)}, s32[23592]{0:T(1024)}, u32[]{:S(2)}) copy-start(s32[23592]{0:T(1024)} %param.18) | copy-start | bytes 283108
  61.6 9.7 %copy-start.4 = (bf16[2,64,1536]{2,1,0:T(8,128)(2,1)S(1)}, bf16[2,64,1536]{2,1,0:T(8,128)(2,1)}, u32[]{:S(2)}) copy-start(bf16[2,64,1536]{2,1,0:T(8,128)(2,1)} %param.17) | copy-start | bytes 1179652
  61.6 11.9 %collective-permute-start = (bf16[2,15,1536]{2,1,0:T(8,128)(2,1)S(1)}, bf16[2,15,1536]{2,1,0:T(8,128)(2,1)S(1)}, u32[]{:S(2)}, u32[]{:S(2)}) collective-permute-start(bf16[2,15,1536]{2,1,0:T(8,128)(2,1)S(1)} %get-tuple-element.70), channel_id=1, source_target_pairs={{0,1},{1,2},{2,3},{3,4},{4,5},{5,6},{6,7},{8,9},{9,10},{10,11},{11... | collective-permute-start | bytes 276488 | tf_op jit(solution)/shard_map/ppermute | solution.py:24
  64.7 6.5 %collective-permute-start.1 = (bf16[2,15,1536]{2,1,0:T(8,128)(2,1)S(1)}, bf16[2,15,1536]{2,1,0:T(8,128)(2,1)S(1)}, u32[]{:S(2)}, u32[]{:S(2)}) collective-permute-start(bf16[2,15,1536]{2,1,0:T(8,128)(2,1)S(1)} %get-tuple-element.71), channel_id=1, source_target_pairs={{1,0},{2,1},{3,2},{4,3},{5,4},{6,5},{7,6},{9,8},{10,9},{11,10},{12... | collective-permute-start | bytes 276488 | tf_op jit(solution)/shard_map/ppermute | solution.py:25

commit v2 on v1

--- a/solution.py
+++ b/solution.py
@@ -72,98 +72,6 @@
     )
     copy.start()
     return copy
-
-
-def attention_kernel(
-    count,
-    score_scale,
-    len_ref,
-    q_ref,
-    k_ref,
-    v_ref,
-    out_ref,
-    send,
-    recv,
-    back,
-    home,
-    send_sem,
-    recv_sem,
-    back_sem,
-    home_sem,
-):
-    utts, frames, width = q_ref.shape
-    block = width // count
-    head_size = width // HEADS
-    me = lax.axis_index("seq")
-    greet((("seq", count),))
-    for owner in range(count):
-        for utt in range(utts):
-            for place, ref in enumerate((q_ref, k_ref, v_ref)):
-                begin = (utt * 3 + place) * block
-                send[owner, :, begin : begin + block] = ref[
-                    utt, :, owner * block : (owner + 1) * block
-                ]
-    copies = [
-        send_to(send.at[peer], recv.at[me], send_sem.at[i], recv_sem.at[i], "seq", peer)
-        for i, peer in enumerate(peers_of("seq", count))
-    ]
-    recv[pl.ds(me, 1)] = send[pl.ds(me, 1)]
-    for copy in copies:
-        copy.wait_recv()
-    full = count * frames
-    ids = lax.broadcasted_iota(jnp.int32, (full, full), 1)
-    for utt in range(utts):
-        key_ok = ids < len_ref[utt]
-        for head in range(block // head_size):
-            parts = []
-            for place in range(3):
-                begin = (utt * 3 + place) * block + head * head_size
-                parts.append(recv[:, :, begin : begin + head_size].reshape(full, head_size))
-            query, key, value = parts
-            scores = lax.dot_general(
-                query, key, (((1,), (1,)), ((), ())), preferred_element_type=jnp.float32
-            )
-            scores = jnp.where(key_ok, scores * score_scale, neg_big)
-            probs = jnp.exp(scores - jnp.max(scores, axis=-1, keepdims=True))
-            denom = jnp.sum(probs, axis=-1, keepdims=True)
-            rows = jnp.dot(probs.astype(jnp.bfloat16), value, preferred_element_type=jnp.float32)
-            rows = (rows / denom).astype(jnp.bfloat16)
-            begin = utt * block + head * head_size
-            back[:, :, begin : begin + head_size] = rows.reshape(count, frames, head_size)
-    returns = [
-        send_to(back.at[peer], home.at[me], back_sem.at[i], home_sem.at[i], "seq", peer)
-        for i, peer in enumerate(peers_of("seq", count))
-    ]
-    home[pl.ds(me, 1)] = back[pl.ds(me, 1)]
-    for copy in returns:
-        copy.wait_recv()
-    for owner in range(count):
-        for utt in range(utts):
-            out_ref[utt, :, owner * block : (owner + 1) * block] = home[
-                owner, :, utt * block : (utt + 1) * block
-            ]
-    for copy in copies + returns:
-        copy.wait_send()
-
-
-def exchanged_attention(queries, key_rows, value_rows, utt_lengths, score_scale):
-    utts, frames, width = queries.shape
-    count = lax.axis_size("seq")
-    block = width // count
-    vmem = pl.BlockSpec(memory_space=pltpu.VMEM)
-    wide = pltpu.VMEM((count, frames, 3 * utts * block), jnp.bfloat16)
-    narrow = pltpu.VMEM((count, frames, utts * block), jnp.bfloat16)
-    sems = pltpu.SemaphoreType.DMA((count - 1,))
-    return pl.pallas_call(
-        functools.partial(attention_kernel, count, score_scale),
-        out_shape=jax.ShapeDtypeStruct(queries.shape, jnp.bfloat16),
-        in_specs=[pl.BlockSpec(memory_space=pltpu.SMEM), vmem, vmem, vmem],
-        out_specs=vmem,
-        scratch_shapes=[wide, wide, narrow, narrow, sems, sems, sems, sems],
-        compiler_params=pltpu.CompilerParams(
-            collective_id=0, has_side_effects=True, vmem_limit_bytes=40 * 2**20
-        ),
-    )(utt_lengths, queries, key_rows, value_rows)
 
 
 def total_kernel(
@@ -310,6 +218,425 @@
     return lax.map(one_utt, (queries, all_keys, all_values, utt_lengths))
 
 
+def shifted_windows(chunk, frames):
+    for turn in range(8):
+        part = chunk[turn : turn + frames + 24]
+        for eight in range(4):
+            offset = 8 * eight + turn
+            if 1 <= offset <= 31:
+                yield offset, part[8 * eight : 8 * eight + frames]
+
+
+def block_kernel(
+    n_seq,
+    n_dp,
+    rows_each,
+    score_scale,
+    norm_factor,
+    len_ref,
+    pick_ref,
+    kern_ref,
+    q_hbm,
+    k_hbm,
+    v_hbm,
+    in_hbm,
+    cot_hbm,
+    w_hbm,
+    conv_ref,
+    cgrad_ref,
+    sum_ref,
+    q_ref,
+    k_ref,
+    v_ref,
+    in_ref,
+    cot_ref,
+    w_ref,
+    send,
+    recv,
+    back,
+    home,
+    cot_edge,
+    hid_edge,
+    cot_pad,
+    hid_pad,
+    hidden,
+    grad,
+    grad_stack,
+    ctx,
+    ctx_stack,
+    grad_picked,
+    kern_grad,
+    x_ref,
+    parts,
+    mine,
+    sums,
+    whole,
+    load_sem,
+    send_sem,
+    recv_sem,
+    back_sem,
+    home_sem,
+    edge_send,
+    edge_recv,
+    s1,
+    r1,
+    s2,
+    r2,
+    s3,
+    r3,
+):
+    utts, frames, width = q_ref.shape
+    taps = kern_ref.shape[0]
+    reach = 16
+    tokens = utts * frames
+    block = width // n_seq
+    head_size = width // HEADS
+    me = lax.axis_index("seq")
+    me_dp = lax.axis_index("dp")
+    right, left = lax.rem(me + 1, n_seq), lax.rem(me + n_seq - 1, n_seq)
+    loads = [
+        pltpu.make_async_copy(src, dst, load_sem.at[i])
+        for i, (src, dst) in enumerate(
+            (
+                (cot_hbm, cot_ref),
+                (q_hbm, q_ref),
+                (k_hbm, k_ref),
+                (v_hbm, v_ref),
+                (w_hbm, w_ref),
+                (in_hbm, in_ref),
+            )
+        )
+    ]
+    for load in loads:
+        load.start()
+    greet((("seq", n_seq), ("dp", n_dp)))
+
+    def swap_edges(rows, edge, base):
+        return [
+            send_to(
+                rows.at[:, frames - reach : frames],
+                edge.at[0],
+                edge_send.at[base],
+                edge_recv.at[base],
+                "seq",
+                right,
+            ),
+            send_to(
+                rows.at[:, 0:reach],
+                edge.at[1],
+                edge_send.at[base + 1],
+                edge_recv.at[base + 1],
+                "seq",
+                left,
+            ),
+        ]
+
+    def pad_edges(edge, pad):
+        for utt in range(utts):
+            before = edge[0, utt].astype(jnp.float32)
+            after = edge[1, utt].astype(jnp.float32)
+            pad[utt, 0:reach, :] = jnp.where(me > 0, before, 0.0)
+            pad[utt, reach + frames : 2 * reach + frames, :] = jnp.where(
+                me < n_seq - 1, after, 0.0
+            )
+
+    for load in loads[:4]:
+        load.wait()
+    for owner in range(n_seq):
+        for utt in range(utts):
+            for place, ref in enumerate((q_ref, k_ref, v_ref)):
+                begin = (utt * 3 + place) * block
+                send[owner, :, begin : begin + block] = ref[
+                    utt, :, owner * block : (owner + 1) * block
+                ]
+    edges = swap_edges(cot_ref, cot_edge, 0)
+    copies = [
+        send_to(send.at[peer], recv.at[me], send_sem.at[i], recv_sem.at[i], "seq", peer)
+        for i, peer in enumerate(peers_of("seq", n_seq))
+    ]
+    recv[pl.ds(me, 1)] = send[pl.ds(me, 1)]
+
+    frame_ids = me * frames + lax.broadcasted_iota(jnp.int32, (frames, 1), 0)
+    for utt in range(utts):
+        cot_pad[utt, reach : reach + frames, :] = cot_ref[utt].astype(jnp.float32)
+    for copy in edges:
+        copy.wait_recv()
+    pad_edges(cot_edge, cot_pad)
+
+    @pl.loop(0, width // 128)
+    def _(step):
+        cols = pl.ds(pl.multiple_of(step * 128, 128), 128)
+        kern = kern_ref[:, cols].astype(jnp.float32)
+        for utt in range(utts):
+            total = jnp.zeros((frames, 128), jnp.float32)
+            for offset, window in shifted_windows(cot_pad[utt, :, cols], frames):
+                tap = taps - offset
+                total = total + kern[tap : tap + 1] * window
+            total = jnp.where(frame_ids < len_ref[utt], total, 0.0)
+            grad[utt * frames : (utt + 1) * frames, cols] = total.astype(jnp.bfloat16)
+
+    for part in range(width // LOW):
+        grad_stack[part * tokens : (part + 1) * tokens, :] = grad[
+            :, part * LOW : (part + 1) * LOW
+        ]
+
+    @pl.loop(0, n_seq)
+    def _(owner):
+        for row in range(rows_each):
+            pick = pick_ref[owner, row : row + 1, :]
+            found = choose(grad_stack[...], tokens, lax.rem(pick, width))
+            grad_picked[owner, row] = found.astype(jnp.bfloat16)
+
+    loads[4].wait()
+    loads[5].wait()
+
+    @pl.loop(0, width // LOW)
+    def _(step):
+        cols = pl.ds(pl.multiple_of(step * LOW, LOW), LOW)
+        value = lax.dot_general(
+            grad[...], w_ref[cols, :], (((1,), (1,)), ((), ())), preferred_element_type=jnp.float32
+        ).astype(jnp.bfloat16)
+        for utt in range(utts):
+            cgrad_ref[utt, :, cols] = value[utt * frames : (utt + 1) * frames]
+
+    for copy in copies:
+        copy.wait_recv()
+    full = n_seq * frames
+    ids = lax.broadcasted_iota(jnp.int32, (full, full), 1)
+    for utt in range(utts):
+        key_ok = ids < len_ref[utt]
+        for head in range(block // head_size):
+            three = []
+            for place in range(3):
+                begin = (utt * 3 + place) * block + head * head_size
+                three.append(recv[:, :, begin : begin + head_size].reshape(full, head_size))
+            query, key, value = three
+            scores = lax.dot_general(
+                query, key, (((1,), (1,)), ((), ())), preferred_element_type=jnp.float32
+            )
+            scores = jnp.where(key_ok, scores * score_scale, neg_big)
+            probs = jnp.exp(scores - jnp.max(scores, axis=-1, keepdims=True))
+            denom = jnp.sum(probs, axis=-1, keepdims=True)
+            rows = jnp.dot(probs.astype(jnp.bfloat16), value, preferred_element_type=jnp.float32)
+            rows = (rows / denom).astype(jnp.bfloat16)
+            begin = utt * block + head * head_size
+            back[:, :, begin : begin + head_size] = rows.reshape(n_seq, frames, head_size)
+    returns = [
+        send_to(back.at[peer], home.at[me], back_sem.at[i], home_sem.at[i], "seq", peer)
+        for i, peer in enumerate(peers_of("seq", n_seq))
+    ]
+    home[pl.ds(me, 1)] = back[pl.ds(me, 1)]
+    for copy in returns:
+        copy.wait_recv()
+    for owner in range(n_seq):
+        for utt in range(utts):
+            ctx[utt * frames : (utt + 1) * frames, owner * block : (owner + 1) * block] = home[
+                owner, :, utt * block : (utt + 1) * block
+            ]
+
+    @pl.loop(0, width // LOW)
+    def _(step):
+        cols = pl.ds(pl.multiple_of(step * LOW, LOW), LOW)
+        value = jnp.dot(ctx[...], w_ref[:, cols], preferred_element_type=jnp.float32)
+        for utt in range(utts):
+            rows = in_ref[utt, :, cols].astype(jnp.float32)
+            rows = rows + value[utt * frames : (utt + 1) * frames]
+            rows = jnp.where(frame_ids < len_ref[utt], rows, 0.0).astype(jnp.bfloat16)
+            hidden[utt, :, cols] = rows
+            hid_pad[utt, reach : reach + frames, cols] = rows.astype(jnp.float32)
+
+    hid_copies = swap_edges(hidden, hid_edge, 2)
+    for part in range(width // LOW):
+        ctx_stack[part * tokens : (part + 1) * tokens, :] = ctx[:, part * LOW : (part + 1) * LOW]
+
+    @pl.loop(0, n_seq)
+    def _(owner):
+        for row in range(rows_each):
+            pick = pick_ref[owner, row : row + 1, :]
+            found = choose(ctx_stack[...], tokens, lax.div(pick, width))
+            found = found * grad_picked[owner, row].astype(jnp.float32)
+            x_ref[owner, row : row + 1, :] = jnp.sum(found, axis=0, keepdims=True)
+
+    for copy in hid_copies:
+        copy.wait_recv()
+    pad_edges(hid_edge, hid_pad)
+    kern_grad[...] = jnp.zeros_like(kern_grad)
+
+    @pl.loop(0, width // 128)
+    def _(step):
+        cols = pl.ds(pl.multiple_of(step * 128, 128), 128)
+        found = {}
+        for utt in range(utts):
+            cot = cot_pad[utt, reach : reach + frames, cols]
+            for offset, window in shifted_windows(hid_pad[utt, :, cols], frames):
+                value = jnp.sum((window * cot).reshape(frames // 8, 8, 128), axis=0)
+                found[offset] = value if utt == 0 else found[offset] + value
+        for offset, value in found.items():
+            kern_grad[offset - 1 : offset, cols] = jnp.sum(value, axis=0, keepdims=True)
+
+    pick = pick_ref[n_seq - 1, rows_each - 1 : rows_each, :]
+    rest = jnp.concatenate(
+        [kern_grad[:, part * LOW : (part + 1) * LOW] for part in range(width // LOW)], axis=0
+    )
+    found = jnp.zeros((kern_grad.shape[0], PICK_TILE), jnp.float32)
+    for _ in range(3):
+        piece = rest.astype(jnp.bfloat16)
+        rest = rest - piece.astype(jnp.float32)
+        found = found + choose(piece, kern_grad.shape[0], lax.rem(pick, width))
+    tap_ids = lax.broadcasted_iota(jnp.int32, found.shape, 0)
+    found = jnp.where(tap_ids == lax.div(pick, width), found, 0.0)
+    x_ref[n_seq - 1, rows_each - 1 : rows_each, :] = jnp.sum(found, axis=0, keepdims=True)
+
+    first = [
+        send_to(x_ref.at[peer], parts.at[me], s1.at[i], r1.at[i], "seq", peer)
+        for i, peer in enumerate(peers_of("seq", n_seq))
+    ]
+    parts[pl.ds(me, 1)] = x_ref[pl.ds(me, 1)]
+
+    @pl.loop(0, width // 128)
+    def _(step):
+        cols = pl.ds(pl.multiple_of(step * 128, 128), 128)
+        kern = kern_ref[:, cols].astype(jnp.float32)
+        for utt in range(utts):
+            total = jnp.zeros((frames, 128), jnp.float32)
+            for offset, window in shifted_windows(hid_pad[utt, :, cols], frames):
+                total = total + kern[offset - 1 : offset] * window
+            conv_ref[utt, :, cols] = total.astype(jnp.bfloat16)
+
+    for copy in first:
+        copy.wait_recv()
+    mine[...] = jnp.sum(parts[...], axis=0)
+    second = [
+        send_to(mine, sums.at[me_dp], s2.at[i], r2.at[i], "dp", peer)
+        for i, peer in enumerate(peers_of("dp", n_dp))
+    ]
+    sums[pl.ds(me_dp, 1)] = mine[...][None]
+    for copy in second:
+        copy.wait_recv()
+    whole[pl.ds(me, 1)] = (jnp.sum(sums[...], axis=0) * norm_factor)[None]
+    third = [
+        send_to(whole.at[me], whole.at[me], s3.at[i], r3.at[i], "seq", peer)
+        for i, peer in enumerate(peers_of("seq", n_seq))
+    ]
+    for copy in third:
+        copy.wait_recv()
+    for owner in range(n_seq):
+        sum_ref[owner * rows_each : (owner + 1) * rows_each] = whole[owner, 0:rows_each]
+    for copy in edges + copies + returns + hid_copies + first + second + third:
+        copy.wait_send()
+
+
+def one_kernel(
+    queries,
+    key_rows,
+    value_rows,
+    layer_input,
+    utt_lengths,
+    out_weight,
+    conv_kernel,
+    conv_cotangent,
+    pick_weight,
+    pick_kernel,
+):
+    utts, frames, width = queries.shape
+    n_seq, n_dp = lax.axis_size("seq"), lax.axis_size("dp")
+    block = width // n_seq
+    tokens = utts * frames
+    tiles = -(-pick_weight.shape[0] // PICK_TILE) + 1
+    rows_each = -(-tiles // n_seq)
+    kernel_start = (rows_each * n_seq - 1) * PICK_TILE
+    picks = jnp.concatenate(
+        [
+            jnp.pad(pick_weight, (0, kernel_start - pick_weight.shape[0])),
+            jnp.pad(pick_kernel, (0, PICK_TILE - pick_kernel.shape[0])),
+        ]
+    ).reshape(n_seq, rows_each, PICK_TILE)
+    held_rows = -(-rows_each // 8) * 8
+    vmem = pl.BlockSpec(memory_space=pltpu.VMEM)
+    hbm = pl.BlockSpec(memory_space=pl.ANY)
+    bf16, f32 = jnp.bfloat16, jnp.float32
+    local = pltpu.VMEM((utts, frames, width), bf16)
+    wide = pltpu.VMEM((n_seq, frames, 3 * utts * block), bf16)
+    narrow = pltpu.VMEM((n_seq, frames, utts * block), bf16)
+    edge = pltpu.VMEM((2, utts, 16, width), bf16)
+    pad = pltpu.VMEM((utts, frames + 32, width), f32)
+    flat = pltpu.VMEM((tokens, width), bf16)
+    stack = pltpu.VMEM((tokens * width // LOW, LOW), bf16)
+    partial = pltpu.VMEM((n_seq, held_rows, PICK_TILE), f32)
+    seq_sems = pltpu.SemaphoreType.DMA((n_seq - 1,))
+    dp_sems = pltpu.SemaphoreType.DMA((n_dp - 1,))
+    score_scale = 1.0 / math.sqrt(width // HEADS)
+    norm_factor = 1.0 / math.sqrt(utts * n_dp * frames * n_seq)
+    conv_out, context_grad, total = pl.pallas_call(
+        functools.partial(block_kernel, n_seq, n_dp, rows_each, score_scale, norm_factor),
+        out_shape=(
+            jax.ShapeDtypeStruct(queries.shape, bf16),
+            jax.ShapeDtypeStruct(queries.shape, bf16),
+            jax.ShapeDtypeStruct((n_seq * rows_each, PICK_TILE), f32),
+        ),
+        in_specs=[pl.BlockSpec(memory_space=pltpu.SMEM), vmem, vmem] + [hbm] * 6,
+        out_specs=(vmem, vmem, vmem),
+        scratch_shapes=[
+            local,
+            local,
+            local,
+            local,
+            local,
+            pltpu.VMEM((width, width), bf16),
+            wide,
+            wide,
+            narrow,
+            narrow,
+            edge,
+            edge,
+            pad,
+            pad,
+            local,
+            flat,
+            stack,
+            flat,
+            stack,
+            pltpu.VMEM((n_seq, rows_each, tokens, PICK_TILE), bf16),
+            pltpu.VMEM((32, width), f32),
+            partial,
+            partial,
+            pltpu.VMEM((held_rows, PICK_TILE), f32),
+            pltpu.VMEM((n_dp, held_rows, PICK_TILE), f32),
+            partial,
+            pltpu.SemaphoreType.DMA((6,)),
+            seq_sems,
+            seq_sems,
+            seq_sems,
+            seq_sems,
+            pltpu.SemaphoreType.DMA((4,)),
+            pltpu.SemaphoreType.DMA((4,)),
+            seq_sems,
+            seq_sems,
+            dp_sems,
+            dp_sems,
+            seq_sems,
+            seq_sems,
+        ],
+        compiler_params=pltpu.CompilerParams(
+            collective_id=2, has_side_effects=True, vmem_limit_bytes=56 * 2**20
+        ),
+    )(
+        utt_lengths,
+        picks,
+        conv_kernel,
+        queries,
+        key_rows,
+        value_rows,
+        layer_input,
+        conv_cotangent,
+        out_weight,
+    )
+    flat_total = total.reshape(-1)
+    weight_picks = flat_total[: pick_weight.shape[0]]
+    kernel_picks = flat_total[kernel_start : kernel_start + pick_kernel.shape[0]]
+    return (conv_out, context_grad, weight_picks, kernel_picks)
+
+
 def on_device(
     queries,
     key_rows,
@@ -324,16 +651,26 @@
 ):
     local_utts, frames_dev, width = queries.shape
     seq_count = lax.axis_size("seq")
+    if HEADS % seq_count == 0:
+        return one_kernel(
+            queries,
+            key_rows,
+            value_rows,
+            layer_input,
+            utt_lengths,
+            out_weight,
+            conv_kernel,
+            conv_cotangent,
+            pick_weight,
+            pick_kernel,
+        )
     full_frames = frames_dev * seq_count
     head_size = width // HEADS
     score_scale = 1.0 / math.sqrt(head_size)
     first_frame = lax.axis_index("seq") * frames_dev
     local_ids = first_frame + jnp.arange(frames_dev, dtype=jnp.int32)
     valid_rows = (local_ids[None, :] < utt_lengths[:, None]).astype(jnp.float32)
-    if HEADS % seq_count == 0:
-        context = exchanged_attention(queries, key_rows, value_rows, utt_lengths, score_scale)
-    else:
-        context = gathered_attention(queries, key_rows, value_rows, utt_lengths, score_scale)
+    context = gathered_attention(queries, key_rows, value_rows, utt_lengths, score_scale)
     context_flat = context.reshape(local_utts * frames_dev, width)
     projected = jnp.dot(context_flat, out_weight, preferred_element_type=jnp.float32).reshape(
         local_utts, frames_dev, width

time: 141 us -> 92 us (0.65)
  other arithmetic: 16.6 us -> 0.92 us
  starting transfers between devices: 10.7 us -> 0 us
  Pallas kernels: 93 us -> 84.4 us
  matrix products: 7.89 us -> 0 us
  waiting for transfers between devices: 4.32 us -> 0 us
    ppermute x4 -> x0, starting transfers between devices: 10.7 us -> none  [the longest x2 7.98 us: padded(): before = lax.ppermute(last, axis, up)]
    pallas_call x3 -> x1, Pallas kernels: 93 us -> 84.4 us  [one_kernel(): pl.pallas_call(functools.partial(block_kernel, n_seq, n_dp, rows_each, sc...]
    convert_element_type x5 -> x0, other arithmetic: 8.45 us -> none  [the longest x1 4.43 us: on_device(): conv_out = conv_sum.astype(jnp.bfloat16)]
    dot_general x2 -> x0, matrix products: 7.89 us -> none  [the longest x1 4.73 us: on_device(): lax.dot_general(grad_flat, out_weight, (((1,), (1,)), ((), ())), preferre...]
    reduce_sum x5 -> x0, other arithmetic: 4.47 us -> none  [the longest x4 4.18 us: on_device(): kernel_rows.append(jnp.sum(window * cot_f, axis=(0, 1)))]
    ppermute x4 -> x0, waiting for transfers between devices: 4.32 us -> none  [the longest x2 4.32 us: padded(): after = lax.ppermute(leading, axis, down)]
    mul x2 -> x0, other arithmetic: 2.79 us -> none  [the longest x1 1.54 us: on_device(): weight_sum * norm_factor]
    unnamed x18 -> x5, local copies, waits for them, and re-layouts: 3.67 us -> 4.46 us
  transfers between devices with their start and end apart: 4 -> 0, of which waited for: 1 -> 0; matrix products, arithmetic and copies ran while one was open for 7% -> 0% of each run, Pallas kernels for 33% -> 0%
where the time goes in v2:
time: 92 us; the launch traced here: 91.7 us
  Pallas kernels  84.4 us (92%)
  local copies, waits for them, and re-layouts  5.73 us (6%)
  other arithmetic  0.92 us (1%)
    pallas_call x1, Pallas kernels, one_kernel(): pl.pallas_call(functools.partial(block_kernel, n_seq, n_dp, rows_each, sc...  84.4 us
    unnamed x5, local copies, waits for them, and re-layouts  4.46 us

profile of v2, /device:TPU:0, one launch (start us, length us, event | category | flops | bytes accessed | tf_op | source)
XLA Modules:
  0.0 91.7 jit_solution(5243003908506997362)
XLA Ops:
  0.6 0.9 %pad_add_fusion = s32[24576]{0:T(1024)S(1)} fusion(s32[476]{0:T(512)} %param.19, s32[23592]{0:T(1024)} %param.18), kind=kLoop, calls=%fused_computation | loop fusion | flops 24576 | bytes 194576 | tf_op jit(solution)/shard_map/concatenate | solution.py:548
  1.6 0.7 reshape.14.pick_ref
  2.2 84.4 %shard_map.129 = (bf16[2,64,1536]{2,1,0:T(8,128)(2,1)}, bf16[2,64,1536]{2,1,0:T(8,128)(2,1)}, f32[48,512]{1,0:T(8,128)}) custom-call(s32[2]{0:T(128)} %len_ref.1, s32[8,6,512]{2,1,0:T(8,128)} %reshape.14.pick_ref, bf16[31,1536]{1,0:T(8,128)(2,1)} %kern_ref.1, bf16[2,64,1536]{2,1,0:T(8,128)(2,1)} %q_hbm.1, bf16[2,64,1536]{2,1,0:T(8,128)(2,1)} %k_hbm.1, ...), custom_call_target="tpu_custom_call" | custom-call | tf_op jit(solution)/shard_map/pallas_call | solution.py:570
  86.7 0.9 %copy.14 = f32[6,4,8,128]{3,1,2,0:T(4,128)S(1)} copy(f32[6,4,8,128]{3,2,1,0:T(8,128)} %bitcast.5) | data formatting | bytes 196608
  87.6 0.0 copy-start
  87.6 0.6 slice.9
  88.2 1.8 %copy.17 = bf16[2,64,1536]{2,1,0:T(8,128)(2,1)} copy(bf16[2,64,1536]{2,1,0:T(8,128)(2,1)} %get-tuple-element.14) | data formatting | bytes 786432
  90.0 1.8 %copy.18 = bf16[2,64,1536]{2,1,0:T(8,128)(2,1)} copy(bf16[2,64,1536]{2,1,0:T(8,128)(2,1)} %get-tuple-element.15) | data formatting | bytes 786432
  91.7 0.0 copy-done
Async XLA Ops:
  87.6 4.1 %copy-start = (f32[6,4,8,128]{3,1,2,0:T(4,128)}, f32[6,4,8,128]{3,1,2,0:T(4,128)S(1)}, u32[]{:S(2)}) copy-start(f32[6,4,8,128]{3,1,2,0:T(4,128)S(1)} %copy.14) | copy-start | bytes 294916

commit v3 on v2

--- a/solution.py
+++ b/solution.py
@@ -287,6 +287,8 @@
 ):
     utts, frames, width = q_ref.shape
     taps = kern_ref.shape[0]
+    lanes = PICK_TILE // 128
+    held = rows_each * lanes
     reach = 16
     tokens = utts * frames
     block = width // n_seq
@@ -311,19 +313,19 @@
         load.start()
     greet((("seq", n_seq), ("dp", n_dp)))
 
-    def swap_edges(rows, edge, base):
+    def swap_edges(rows, edge, utt, base):
         return [
             send_to(
-                rows.at[:, frames - reach : frames],
-                edge.at[0],
+                rows.at[utt, frames - reach : frames],
+                edge.at[0, utt],
                 edge_send.at[base],
                 edge_recv.at[base],
                 "seq",
                 right,
             ),
             send_to(
-                rows.at[:, 0:reach],
-                edge.at[1],
+                rows.at[utt, 0:reach],
+                edge.at[1, utt],
                 edge_send.at[base + 1],
                 edge_recv.at[base + 1],
                 "seq",
@@ -340,21 +342,124 @@
                 me < n_seq - 1, after, 0.0
             )
 
+    half = frames // 2
+
+    def send_heads(utt):
+        for owner in range(n_seq):
+            for part in range(2):
+                for place, ref in enumerate((q_ref, k_ref, v_ref)):
+                    begin = (part * 3 + place) * block
+                    send[utt, owner, :, begin : begin + block] = ref[
+                        utt, part * half : (part + 1) * half, owner * block : (owner + 1) * block
+                    ]
+        sent = [
+            send_to(
+                send.at[utt, peer],
+                recv.at[utt, me],
+                send_sem.at[utt, i],
+                recv_sem.at[utt, i],
+                "seq",
+                peer,
+            )
+            for i, peer in enumerate(peers_of("seq", n_seq))
+        ]
+        recv[utt, pl.ds(me, 1)] = send[utt, pl.ds(me, 1)]
+        return sent
+
+    def attend(utt):
+        full = n_seq * frames
+        key_ok = lax.broadcasted_iota(jnp.int32, (full, full), 1) < len_ref[utt]
+        for head in range(block // head_size):
+            three = []
+            for place in range(3):
+                pieces = []
+                for part in range(2):
+                    begin = (part * 3 + place) * block + head * head_size
+                    pieces.append(recv[utt, :, :, begin : begin + head_size])
+                three.append(jnp.concatenate(pieces, axis=1).reshape(full, head_size))
+            query, key, value = three
+            scores = lax.dot_general(
+                query, key, (((1,), (1,)), ((), ())), preferred_element_type=jnp.float32
+            )
+            scores = jnp.where(key_ok, scores * score_scale, neg_big)
+            probs = jnp.exp(scores - jnp.max(scores, axis=-1, keepdims=True))
+            denom = jnp.sum(probs, axis=-1, keepdims=True)
+            rows = jnp.dot(probs.astype(jnp.bfloat16), value, preferred_element_type=jnp.float32)
+            rows = (rows / denom).astype(jnp.bfloat16).reshape(n_seq, frames, head_size)
+            for part in range(2):
+                begin = part * block + head * head_size
+                back[utt, :, :, begin : begin + head_size] = rows[
+                    :, part * half : (part + 1) * half
+                ]
+        sent = [
+            send_to(
+                back.at[utt, peer],
+                home.at[utt, me],
+                back_sem.at[utt, i],
+                home_sem.at[utt, i],
+                "seq",
+                peer,
+            )
+            for i, peer in enumerate(peers_of("seq", n_seq))
+        ]
+        home[utt, pl.ds(me, 1)] = back[utt, pl.ds(me, 1)]
+        return sent
+
+    def project(utt):
+        first_row = utt * frames
+        for owner in range(n_seq):
+            for part in range(2):
+                rows = slice(first_row + part * half, first_row + (part + 1) * half)
+                ctx[rows, owner * block : (owner + 1) * block] = home[
+                    utt, owner, :, part * block : (part + 1) * block
+                ]
+        rows = slice(first_row, first_row + frames)
+
+        @pl.loop(0, width // LOW)
+        def _(step):
+            cols = pl.ds(pl.multiple_of(step * LOW, LOW), LOW)
+            value = jnp.dot(ctx[rows, :], w_ref[:, cols], preferred_element_type=jnp.float32)
+            value = in_ref[utt, :, cols].astype(jnp.float32) + value
+            value = jnp.where(frame_ids < len_ref[utt], value, 0.0).astype(jnp.bfloat16)
+            hidden[utt, :, cols] = value
+            hid_pad[utt, reach : reach + frames, cols] = value.astype(jnp.float32)
+
+        sent = swap_edges(hidden, hid_edge, utt, 2 * utts + 2 * utt)
+        for part in range(width // LOW):
+            ctx_stack[utt, part * frames : (part + 1) * frames, :] = ctx[
+                rows, part * LOW : (part + 1) * LOW
+            ]
+        return sent
+
+    def pick_context(utt):
+        @pl.loop(0, n_seq)
+        def _(owner):
+            for row in range(rows_each):
+                found = choose(ctx_stack[utt], frames, lax.div(pick_row(owner, row), width))
+                other = grad_picked[owner, row, utt * frames : (utt + 1) * frames, :]
+                found = jnp.sum(found * other.astype(jnp.float32), axis=0, keepdims=True)
+                store_row(owner, row, found, utt > 0)
+
+    def pick_row(owner, row):
+        return jnp.concatenate(
+            [pick_ref[owner, lanes * row + i : lanes * row + i + 1, :] for i in range(lanes)],
+            axis=1,
+        )
+
+    def store_row(owner, row, value, add):
+        for i in range(lanes):
+            place = slice(lanes * row + i, lanes * row + i + 1)
+            piece = value[:, i * 128 : (i + 1) * 128]
+            if add:
+                piece = piece + x_ref[owner, place, :]
+            x_ref[owner, place, :] = piece
+
     for load in loads[:4]:
         load.wait()
-    for owner in range(n_seq):
-        for utt in range(utts):
-            for place, ref in enumerate((q_ref, k_ref, v_ref)):
-                begin = (utt * 3 + place) * block
-                send[owner, :, begin : begin + block] = ref[
-                    utt, :, owner * block : (owner + 1) * block
-                ]
-    edges = swap_edges(cot_ref, cot_edge, 0)
-    copies = [
-        send_to(send.at[peer], recv.at[me], send_sem.at[i], recv_sem.at[i], "seq", peer)
-        for i, peer in enumerate(peers_of("seq", n_seq))
-    ]
-    recv[pl.ds(me, 1)] = send[pl.ds(me, 1)]
+    copies = send_heads(0)
+    edges = []
+    for utt in range(utts):
+        edges += swap_edges(cot_ref, cot_edge, utt, 2 * utt)
 
     frame_ids = me * frames + lax.broadcasted_iota(jnp.int32, (frames, 1), 0)
     for utt in range(utts):
@@ -380,83 +485,44 @@
             :, part * LOW : (part + 1) * LOW
         ]
 
-    @pl.loop(0, n_seq)
-    def _(owner):
-        for row in range(rows_each):
-            pick = pick_ref[owner, row : row + 1, :]
-            found = choose(grad_stack[...], tokens, lax.rem(pick, width))
-            grad_picked[owner, row] = found.astype(jnp.bfloat16)
-
-    loads[4].wait()
-    loads[5].wait()
-
-    @pl.loop(0, width // LOW)
-    def _(step):
-        cols = pl.ds(pl.multiple_of(step * LOW, LOW), LOW)
-        value = lax.dot_general(
-            grad[...], w_ref[cols, :], (((1,), (1,)), ((), ())), preferred_element_type=jnp.float32
-        ).astype(jnp.bfloat16)
-        for utt in range(utts):
-            cgrad_ref[utt, :, cols] = value[utt * frames : (utt + 1) * frames]
-
-    for copy in copies:
-        copy.wait_recv()
-    full = n_seq * frames
-    ids = lax.broadcasted_iota(jnp.int32, (full, full), 1)
+    def pick_grad(begin, end):
+        @pl.loop(begin, end)
+        def _(owner):
+            for row in range(rows_each):
+                found = choose(grad_stack[...], tokens, lax.rem(pick_row(owner, row), width))
+                grad_picked[owner, row] = found.astype(jnp.bfloat16)
+
+    pick_grad(0, n_seq // 2)
+    for utt in range(1, utts):
+        copies += send_heads(utt)
+    pick_grad(n_seq // 2, n_seq)
+    returns = []
     for utt in range(utts):
-        key_ok = ids < len_ref[utt]
-        for head in range(block // head_size):
-            three = []
-            for place in range(3):
-                begin = (utt * 3 + place) * block + head * head_size
-                three.append(recv[:, :, begin : begin + head_size].reshape(full, head_size))
-            query, key, value = three
-            scores = lax.dot_general(
-                query, key, (((1,), (1,)), ((), ())), preferred_element_type=jnp.float32
-            )
-            scores = jnp.where(key_ok, scores * score_scale, neg_big)
-            probs = jnp.exp(scores - jnp.max(scores, axis=-1, keepdims=True))
-            denom = jnp.sum(probs, axis=-1, keepdims=True)
-            rows = jnp.dot(probs.astype(jnp.bfloat16), value, preferred_element_type=jnp.float32)
-            rows = (rows / denom).astype(jnp.bfloat16)
-            begin = utt * block + head * head_size
-            back[:, :, begin : begin + head_size] = rows.reshape(n_seq, frames, head_size)
-    returns = [
-        send_to(back.at[peer], home.at[me], back_sem.at[i], home_sem.at[i], "seq", peer)
-        for i, peer in enumerate(peers_of("seq", n_seq))
-    ]
-    home[pl.ds(me, 1)] = back[pl.ds(me, 1)]
-    for copy in returns:
-        copy.wait_recv()
-    for owner in range(n_seq):
-        for utt in range(utts):
-            ctx[utt * frames : (utt + 1) * frames, owner * block : (owner + 1) * block] = home[
-                owner, :, utt * block : (utt + 1) * block
-            ]
-
-    @pl.loop(0, width // LOW)
-    def _(step):
-        cols = pl.ds(pl.multiple_of(step * LOW, LOW), LOW)
-        value = jnp.dot(ctx[...], w_ref[:, cols], preferred_element_type=jnp.float32)
-        for utt in range(utts):
-            rows = in_ref[utt, :, cols].astype(jnp.float32)
-            rows = rows + value[utt * frames : (utt + 1) * frames]
-            rows = jnp.where(frame_ids < len_ref[utt], rows, 0.0).astype(jnp.bfloat16)
-            hidden[utt, :, cols] = rows
-            hid_pad[utt, reach : reach + frames, cols] = rows.astype(jnp.float32)
-
-    hid_copies = swap_edges(hidden, hid_edge, 2)
-    for part in range(width // LOW):
-        ctx_stack[part * tokens : (part + 1) * tokens, :] = ctx[:, part * LOW : (part + 1) * LOW]
-
-    @pl.loop(0, n_seq)
-    def _(owner):
-        for row in range(rows_each):
-            pick = pick_ref[owner, row : row + 1, :]
-            found = choose(ctx_stack[...], tokens, lax.div(pick, width))
-            found = found * grad_picked[owner, row].astype(jnp.float32)
-            x_ref[owner, row : row + 1, :] = jnp.sum(found, axis=0, keepdims=True)
-
+        for copy in copies[utt * (n_seq - 1) : (utt + 1) * (n_seq - 1)]:
+            copy.wait_recv()
+        returns += attend(utt)
+        if utt == 0:
+            loads[4].wait()
+            loads[5].wait()
+
+            @pl.loop(0, width // LOW)
+            def _(step):
+                cols = pl.ds(pl.multiple_of(step * LOW, LOW), LOW)
+                value = lax.dot_general(
+                    grad[...],
+                    w_ref[cols, :],
+                    (((1,), (1,)), ((), ())),
+                    preferred_element_type=jnp.float32,
+                ).astype(jnp.bfloat16)
+                for row in range(utts):
+                    cgrad_ref[row, :, cols] = value[row * frames : (row + 1) * frames]
+
+    hid_copies = []
+    for utt in range(utts):
+        for copy in returns[utt * (n_seq - 1) : (utt + 1) * (n_seq - 1)]:
+            copy.wait_recv()
+        hid_copies += project(utt)
+        pick_context(utt)
     for copy in hid_copies:
         copy.wait_recv()
     pad_edges(hid_edge, hid_pad)
@@ -474,7 +540,7 @@
         for offset, value in found.items():
             kern_grad[offset - 1 : offset, cols] = jnp.sum(value, axis=0, keepdims=True)
 
-    pick = pick_ref[n_seq - 1, rows_each - 1 : rows_each, :]
+    pick = pick_row(n_seq - 1, rows_each - 1)
     rest = jnp.concatenate(
         [kern_grad[:, part * LOW : (part + 1) * LOW] for part in range(width // LOW)], axis=0
     )
@@ -485,7 +551,7 @@
         found = found + choose(piece, kern_grad.shape[0], lax.rem(pick, width))
     tap_ids = lax.broadcasted_iota(jnp.int32, found.shape, 0)
     found = jnp.where(tap_ids == lax.div(pick, width), found, 0.0)
-    x_ref[n_seq - 1, rows_each - 1 : rows_each, :] = jnp.sum(found, axis=0, keepdims=True)
+    store_row(n_seq - 1, rows_each - 1, jnp.sum(found, axis=0, keepdims=True), False)
 
     first = [
         send_to(x_ref.at[peer], parts.at[me], s1.at[i], r1.at[i], "seq", peer)
@@ -493,16 +559,19 @@
     ]
     parts[pl.ds(me, 1)] = x_ref[pl.ds(me, 1)]
 
-    @pl.loop(0, width // 128)
-    def _(step):
-        cols = pl.ds(pl.multiple_of(step * 128, 128), 128)
-        kern = kern_ref[:, cols].astype(jnp.float32)
-        for utt in range(utts):
-            total = jnp.zeros((frames, 128), jnp.float32)
-            for offset, window in shifted_windows(hid_pad[utt, :, cols], frames):
-                total = total + kern[offset - 1 : offset] * window
-            conv_ref[utt, :, cols] = total.astype(jnp.bfloat16)
-
+    def convolve(begin, end):
+        @pl.loop(begin, end)
+        def _(step):
+            cols = pl.ds(pl.multiple_of(step * 128, 128), 128)
+            kern = kern_ref[:, cols].astype(jnp.float32)
+            for utt in range(utts):
+                total = jnp.zeros((frames, 128), jnp.float32)
+                for offset, window in shifted_windows(hid_pad[utt, :, cols], frames):
+                    total = total + kern[offset - 1 : offset] * window
+                conv_ref[utt, :, cols] = total.astype(jnp.bfloat16)
+
+    third_part = width // 128 // 3
+    convolve(0, third_part)
     for copy in first:
         copy.wait_recv()
     mine[...] = jnp.sum(parts[...], axis=0)
@@ -511,6 +580,7 @@
         for i, peer in enumerate(peers_of("dp", n_dp))
     ]
     sums[pl.ds(me_dp, 1)] = mine[...][None]
+    convolve(third_part, 2 * third_part)
     for copy in second:
         copy.wait_recv()
     whole[pl.ds(me, 1)] = (jnp.sum(sums[...], axis=0) * norm_factor)[None]
@@ -518,12 +588,37 @@
         send_to(whole.at[me], whole.at[me], s3.at[i], r3.at[i], "seq", peer)
         for i, peer in enumerate(peers_of("seq", n_seq))
     ]
+    convolve(2 * third_part, width // 128)
     for copy in third:
         copy.wait_recv()
     for owner in range(n_seq):
-        sum_ref[owner * rows_each : (owner + 1) * rows_each] = whole[owner, 0:rows_each]
+        sum_ref[owner * held : (owner + 1) * held] = whole[owner]
     for copy in edges + copies + returns + hid_copies + first + second + third:
         copy.wait_send()
+
+
+def write_kernel(*refs):
+    count = len(refs) // 2
+    sems = refs[-1]
+    copies = [
+        pltpu.make_async_copy(refs[i], refs[count + i], sems.at[i]) for i in range(count)
+    ]
+    for copy in copies:
+        copy.start()
+    for copy in copies:
+        copy.wait()
+
+
+def written(*arrays):
+    spec = pl.BlockSpec(memory_space=pl.ANY)
+    return pl.pallas_call(
+        write_kernel,
+        out_shape=[jax.ShapeDtypeStruct(array.shape, array.dtype) for array in arrays],
+        in_specs=[spec] * len(arrays),
+        out_specs=[spec] * len(arrays),
+        scratch_shapes=[pltpu.SemaphoreType.DMA((len(arrays),))],
+        compiler_params=pltpu.CompilerParams(vmem_limit_bytes=56 * 2**20),
+    )(*arrays)
 
 
 def one_kernel(
@@ -543,28 +638,29 @@
     block = width // n_seq
     tokens = utts * frames
     tiles = -(-pick_weight.shape[0] // PICK_TILE) + 1
-    rows_each = -(-tiles // n_seq)
+    rows_each = -(-tiles // (2 * n_seq)) * 2
+    held_rows = rows_each * PICK_TILE // 128
     kernel_start = (rows_each * n_seq - 1) * PICK_TILE
     picks = jnp.concatenate(
         [
             jnp.pad(pick_weight, (0, kernel_start - pick_weight.shape[0])),
             jnp.pad(pick_kernel, (0, PICK_TILE - pick_kernel.shape[0])),
         ]
-    ).reshape(n_seq, rows_each, PICK_TILE)
-    held_rows = -(-rows_each // 8) * 8
+    ).reshape(n_seq, held_rows, 128)
     vmem = pl.BlockSpec(memory_space=pltpu.VMEM)
     hbm = pl.BlockSpec(memory_space=pl.ANY)
     bf16, f32 = jnp.bfloat16, jnp.float32
     local = pltpu.VMEM((utts, frames, width), bf16)
-    wide = pltpu.VMEM((n_seq, frames, 3 * utts * block), bf16)
-    narrow = pltpu.VMEM((n_seq, frames, utts * block), bf16)
+    wide = pltpu.VMEM((utts, n_seq, frames // 2, 6 * block), bf16)
+    narrow = pltpu.VMEM((utts, n_seq, frames // 2, 2 * block), bf16)
     edge = pltpu.VMEM((2, utts, 16, width), bf16)
     pad = pltpu.VMEM((utts, frames + 32, width), f32)
     flat = pltpu.VMEM((tokens, width), bf16)
     stack = pltpu.VMEM((tokens * width // LOW, LOW), bf16)
-    partial = pltpu.VMEM((n_seq, held_rows, PICK_TILE), f32)
+    partial = pltpu.VMEM((n_seq, held_rows, 128), f32)
     seq_sems = pltpu.SemaphoreType.DMA((n_seq - 1,))
     dp_sems = pltpu.SemaphoreType.DMA((n_dp - 1,))
+    utt_sems = pltpu.SemaphoreType.DMA((utts, n_seq - 1))
     score_scale = 1.0 / math.sqrt(width // HEADS)
     norm_factor = 1.0 / math.sqrt(utts * n_dp * frames * n_seq)
     conv_out, context_grad, total = pl.pallas_call(
@@ -572,7 +668,7 @@
         out_shape=(
             jax.ShapeDtypeStruct(queries.shape, bf16),
             jax.ShapeDtypeStruct(queries.shape, bf16),
-            jax.ShapeDtypeStruct((n_seq * rows_each, PICK_TILE), f32),
+            jax.ShapeDtypeStruct((n_seq * held_rows, 128), f32),
         ),
         in_specs=[pl.BlockSpec(memory_space=pltpu.SMEM), vmem, vmem] + [hbm] * 6,
         out_specs=(vmem, vmem, vmem),
@@ -595,21 +691,21 @@
             flat,
             stack,
             flat,
-            stack,
+            pltpu.VMEM((utts, frames * width // LOW, LOW), bf16),
             pltpu.VMEM((n_seq, rows_each, tokens, PICK_TILE), bf16),
             pltpu.VMEM((32, width), f32),
             partial,
             partial,
-            pltpu.VMEM((held_rows, PICK_TILE), f32),
-            pltpu.VMEM((n_dp, held_rows, PICK_TILE), f32),
+            pltpu.VMEM((held_rows, 128), f32),
+            pltpu.VMEM((n_dp, held_rows, 128), f32),
             partial,
             pltpu.SemaphoreType.DMA((6,)),
-            seq_sems,
-            seq_sems,
-            seq_sems,
-            seq_sems,
-            pltpu.SemaphoreType.DMA((4,)),
-            pltpu.SemaphoreType.DMA((4,)),
+            utt_sems,
+            utt_sems,
+            utt_sems,
+            utt_sems,
+            pltpu.SemaphoreType.DMA((4 * utts,)),
+            pltpu.SemaphoreType.DMA((4 * utts,)),
             seq_sems,
             seq_sems,
             dp_sems,
@@ -631,6 +727,7 @@
         conv_cotangent,
         out_weight,
     )
+    conv_out, context_grad, total = written(conv_out, context_grad, total)
     flat_total = total.reshape(-1)
     weight_picks = flat_total[: pick_weight.shape[0]]
     kernel_picks = flat_total[kernel_start : kernel_start + pick_kernel.shape[0]]

time: 92 us -> 123 us (1.34)
  Pallas kernels: 84.4 us -> 119 us
  local copies, waits for them, and re-layouts: 5.73 us -> 1.27 us
    pallas_call x0 -> x1, Pallas kernels: none -> 27.9 us  [written(): pl.pallas_call(write_kernel, out_shape=[jax.ShapeDtypeStruct(array.shape,...]
    pallas_call x1, Pallas kernels: 84.4 us -> 91.5 us  [one_kernel(): pl.pallas_call(functools.partial(block_kernel, n_seq, n_dp, rows_each, sc...]
    unnamed x5 -> x0, local copies, waits for them, and re-layouts: 4.46 us -> none
where the time goes in v3:
time: 123 us
  Pallas kernels  119 us (97%)
  other arithmetic  1.56 us (1%)
  local copies, waits for them, and re-layouts  1.27 us (1%)
    pallas_call x1, Pallas kernels, one_kernel(): pl.pallas_call(functools.partial(block_kernel, n_seq, n_dp, rows_each, sc...  91.5 us
    pallas_call x1, Pallas kernels, written(): pl.pallas_call(write_kernel, out_shape=[jax.ShapeDtypeStruct(array.shape,...  27.9 us

profile of v3, /device:TPU:0, one launch (start us, length us, event | category | flops | bytes accessed | tf_op | source)
XLA Modules:
  0.0 122.9 jit_solution(9593826355643710355)
XLA Ops:
  0.6 1.6 %pad_add_fusion = s32[24576]{0:T(1024)} fusion(s32[476]{0:T(512)} %param.19, s32[23592]{0:T(1024)} %param.18), kind=kLoop, calls=%fused_computation | loop fusion | flops 24576 | bytes 194576 | tf_op jit(solution)/shard_map/concatenate | solution.py:644
  2.2 91.5 %shard_map.129 = (bf16[2,64,1536]{2,1,0:T(8,128)(2,1)}, bf16[2,64,1536]{2,1,0:T(8,128)(2,1)}, f32[192,128]{1,0:T(8,128)}) custom-call(s32[2]{0:T(128)} %len_ref.1, s32[8,24,128]{2,1,0:T(8,128)} %bitcast.3, bf16[31,1536]{1,0:T(8,128)(2,1)} %kern_ref.1, bf16[2,64,1536]{2,1,0:T(8,128)(2,1)} %q_hbm.1, bf16[2,64,1536]{2,1,0:T(8,128)(2,1)} %k_hbm.1, ...), custom_call_target="tpu_custom_call" | custom-call | tf_op jit(solution)/shard_map/pallas_call | solution.py:666
  93.7 27.9 %shard_map.130 = (bf16[2,64,1536]{2,1,0:T(8,128)(2,1)}, bf16[2,64,1536]{2,1,0:T(8,128)(2,1)}, f32[192,128]{1,0:T(8,128)}) custom-call(bf16[2,64,1536]{2,1,0:T(8,128)(2,1)} %get-tuple-element.10.refs_0_, bf16[2,64,1536]{2,1,0:T(8,128)(2,1)} %get-tuple-element.11.refs_1_, f32[192,128]{1,0:T(8,128)} %get-tuple-element.12.refs_2_), custom_call_target="tpu_custom_call" | custom-call | tf_op jit(solution)/shard_map/pallas_call | solution.py:614
  121.6 1.3 %slice.9 = f32[476]{0:T(512)} slice(f32[24576]{0:T(1024)} %bitcast.4), slice={[24064:24540]} | slice | bytes 3808 | tf_op jit(solution)/shard_map/slice | solution.py:733

commit v4 on v3

--- a/solution.py
+++ b/solution.py
@@ -144,8 +144,9 @@
 def choose(stacked, tokens, index):
     low = lax.rem(index, LOW)
     high = lax.div(index, LOW)
-    hot = lax.broadcasted_iota(jnp.int32, (LOW, index.shape[1]), 0) == low
-    hot = jnp.where(hot, 1.0, 0.0).astype(jnp.bfloat16)
+    ids = lax.broadcasted_iota(jnp.int32, (LOW, index.shape[1]), 0).astype(jnp.bfloat16)
+    one, zero = jnp.bfloat16(1.0), jnp.bfloat16(0.0)
+    hot = jnp.where(ids == low.astype(jnp.bfloat16), one, zero)
     every = jnp.dot(stacked, hot, preferred_element_type=jnp.float32)
     out = every[:tokens]
     for part in range(1, stacked.shape[0] // tokens):
@@ -245,6 +246,7 @@
     conv_ref,
     cgrad_ref,
     sum_ref,
+    tile_ref,
     q_ref,
     k_ref,
     v_ref,
@@ -271,6 +273,10 @@
     mine,
     sums,
     whole,
+    tile,
+    tile_parts,
+    tile_mine,
+    tile_sums,
     load_sem,
     send_sem,
     recv_sem,
@@ -284,6 +290,10 @@
     r2,
     s3,
     r3,
+    s4,
+    r4,
+    s5,
+    r5,
 ):
     utts, frames, width = q_ref.shape
     taps = kern_ref.shape[0]
@@ -426,19 +436,17 @@
 
         sent = swap_edges(hidden, hid_edge, utt, 2 * utts + 2 * utt)
         for part in range(width // LOW):
-            ctx_stack[utt, part * frames : (part + 1) * frames, :] = ctx[
-                rows, part * LOW : (part + 1) * LOW
-            ]
+            begin = part * tokens + first_row
+            ctx_stack[begin : begin + frames, :] = ctx[rows, part * LOW : (part + 1) * LOW]
         return sent
 
-    def pick_context(utt):
+    def pick_context():
         @pl.loop(0, n_seq)
         def _(owner):
             for row in range(rows_each):
-                found = choose(ctx_stack[utt], frames, lax.div(pick_row(owner, row), width))
-                other = grad_picked[owner, row, utt * frames : (utt + 1) * frames, :]
-                found = jnp.sum(found * other.astype(jnp.float32), axis=0, keepdims=True)
-                store_row(owner, row, found, utt > 0)
+                found = choose(ctx_stack[...], tokens, lax.div(pick_row(owner, row), width))
+                found = found * grad_picked[owner, row].astype(jnp.float32)
+                store_row(x_ref.at[owner], row, jnp.sum(found, axis=0, keepdims=True))
 
     def pick_row(owner, row):
         return jnp.concatenate(
@@ -446,13 +454,10 @@
             axis=1,
         )
 
-    def store_row(owner, row, value, add):
+    def store_row(ref, row, value):
         for i in range(lanes):
             place = slice(lanes * row + i, lanes * row + i + 1)
-            piece = value[:, i * 128 : (i + 1) * 128]
-            if add:
-                piece = piece + x_ref[owner, place, :]
-            x_ref[owner, place, :] = piece
+            ref[place, :] = value[:, i * 128 : (i + 1) * 128]
 
     for load in loads[:4]:
         load.wait()
@@ -492,37 +497,37 @@
                 found = choose(grad_stack[...], tokens, lax.rem(pick_row(owner, row), width))
                 grad_picked[owner, row] = found.astype(jnp.bfloat16)
 
-    pick_grad(0, n_seq // 2)
     for utt in range(1, utts):
         copies += send_heads(utt)
-    pick_grad(n_seq // 2, n_seq)
+    pick_grad(0, n_seq)
     returns = []
     for utt in range(utts):
         for copy in copies[utt * (n_seq - 1) : (utt + 1) * (n_seq - 1)]:
             copy.wait_recv()
         returns += attend(utt)
-        if utt == 0:
-            loads[4].wait()
-            loads[5].wait()
-
-            @pl.loop(0, width // LOW)
-            def _(step):
-                cols = pl.ds(pl.multiple_of(step * LOW, LOW), LOW)
-                value = lax.dot_general(
-                    grad[...],
-                    w_ref[cols, :],
-                    (((1,), (1,)), ((), ())),
-                    preferred_element_type=jnp.float32,
-                ).astype(jnp.bfloat16)
-                for row in range(utts):
-                    cgrad_ref[row, :, cols] = value[row * frames : (row + 1) * frames]
+    loads[4].wait()
+    loads[5].wait()
+
+    @pl.loop(0, width // LOW)
+    def _(step):
+        cols = pl.ds(pl.multiple_of(step * LOW, LOW), LOW)
+        value = lax.dot_general(
+            grad[...], w_ref[cols, :], (((1,), (1,)), ((), ())), preferred_element_type=jnp.float32
+        ).astype(jnp.bfloat16)
+        for row in range(utts):
+            cgrad_ref[row, :, cols] = value[row * frames : (row + 1) * frames]
 
     hid_copies = []
     for utt in range(utts):
         for copy in returns[utt * (n_seq - 1) : (utt + 1) * (n_seq - 1)]:
             copy.wait_recv()
         hid_copies += project(utt)
-        pick_context(utt)
+    pick_context()
+    first = [
+        send_to(x_ref.at[peer], parts.at[me], s1.at[i], r1.at[i], "seq", peer)
+        for i, peer in enumerate(peers_of("seq", n_seq))
+    ]
+    parts[pl.ds(me, 1)] = x_ref[pl.ds(me, 1)]
     for copy in hid_copies:
         copy.wait_recv()
     pad_edges(hid_edge, hid_pad)
@@ -551,13 +556,14 @@
         found = found + choose(piece, kern_grad.shape[0], lax.rem(pick, width))
     tap_ids = lax.broadcasted_iota(jnp.int32, found.shape, 0)
     found = jnp.where(tap_ids == lax.div(pick, width), found, 0.0)
-    store_row(n_seq - 1, rows_each - 1, jnp.sum(found, axis=0, keepdims=True), False)
-
-    first = [
-        send_to(x_ref.at[peer], parts.at[me], s1.at[i], r1.at[i], "seq", peer)
+    tile[...] = jnp.zeros_like(tile)
+    store_row(tile, 0, jnp.sum(found, axis=0, keepdims=True))
+
+    tile_first = [
+        send_to(tile, tile_parts.at[me], s4.at[i], r4.at[i], "seq", peer)
         for i, peer in enumerate(peers_of("seq", n_seq))
     ]
-    parts[pl.ds(me, 1)] = x_ref[pl.ds(me, 1)]
+    tile_parts[pl.ds(me, 1)] = tile[...][None]
 
     def convolve(begin, end):
         @pl.loop(begin, end)
@@ -571,7 +577,6 @@
                 conv_ref[utt, :, cols] = total.astype(jnp.bfloat16)
 
     third_part = width // 128 // 3
-    convolve(0, third_part)
     for copy in first:
         copy.wait_recv()
     mine[...] = jnp.sum(parts[...], axis=0)
@@ -580,7 +585,15 @@
         for i, peer in enumerate(peers_of("dp", n_dp))
     ]
     sums[pl.ds(me_dp, 1)] = mine[...][None]
-    convolve(third_part, 2 * third_part)
+    convolve(0, third_part)
+    for copy in tile_first:
+        copy.wait_recv()
+    tile_mine[...] = jnp.sum(tile_parts[...], axis=0)
+    tile_second = [
+        send_to(tile_mine, tile_sums.at[me_dp], s5.at[i], r5.at[i], "dp", peer)
+        for i, peer in enumerate(peers_of("dp", n_dp))
+    ]
+    tile_sums[pl.ds(me_dp, 1)] = tile_mine[...][None]
     for copy in second:
         copy.wait_recv()
     whole[pl.ds(me, 1)] = (jnp.sum(sums[...], axis=0) * norm_factor)[None]
@@ -588,37 +601,18 @@
         send_to(whole.at[me], whole.at[me], s3.at[i], r3.at[i], "seq", peer)
         for i, peer in enumerate(peers_of("seq", n_seq))
     ]
-    convolve(2 * third_part, width // 128)
+    convolve(third_part, width // 128)
+    for copy in tile_second:
+        copy.wait_recv()
+    tile_ref[...] = jnp.sum(tile_sums[...], axis=0) * norm_factor
     for copy in third:
         copy.wait_recv()
     for owner in range(n_seq):
         sum_ref[owner * held : (owner + 1) * held] = whole[owner]
     for copy in edges + copies + returns + hid_copies + first + second + third:
         copy.wait_send()
-
-
-def write_kernel(*refs):
-    count = len(refs) // 2
-    sems = refs[-1]
-    copies = [
-        pltpu.make_async_copy(refs[i], refs[count + i], sems.at[i]) for i in range(count)
-    ]
-    for copy in copies:
-        copy.start()
-    for copy in copies:
-        copy.wait()
-
-
-def written(*arrays):
-    spec = pl.BlockSpec(memory_space=pl.ANY)
-    return pl.pallas_call(
-        write_kernel,
-        out_shape=[jax.ShapeDtypeStruct(array.shape, array.dtype) for array in arrays],
-        in_specs=[spec] * len(arrays),
-        out_specs=[spec] * len(arrays),
-        scratch_shapes=[pltpu.SemaphoreType.DMA((len(arrays),))],
-        compiler_params=pltpu.CompilerParams(vmem_limit_bytes=56 * 2**20),
-    )(*arrays)
+    for copy in tile_first + tile_second:
+        copy.wait_send()
 
 
 def one_kernel(
@@ -663,15 +657,16 @@
     utt_sems = pltpu.SemaphoreType.DMA((utts, n_seq - 1))
     score_scale = 1.0 / math.sqrt(width // HEADS)
     norm_factor = 1.0 / math.sqrt(utts * n_dp * frames * n_seq)
-    conv_out, context_grad, total = pl.pallas_call(
+    conv_out, context_grad, total, tile = pl.pallas_call(
         functools.partial(block_kernel, n_seq, n_dp, rows_each, score_scale, norm_factor),
         out_shape=(
             jax.ShapeDtypeStruct(queries.shape, bf16),
             jax.ShapeDtypeStruct(queries.shape, bf16),
             jax.ShapeDtypeStruct((n_seq * held_rows, 128), f32),
+            jax.ShapeDtypeStruct((8, 128), f32),
         ),
         in_specs=[pl.BlockSpec(memory_space=pltpu.SMEM), vmem, vmem] + [hbm] * 6,
-        out_specs=(vmem, vmem, vmem),
+        out_specs=(vmem, vmem, vmem, vmem),
         scratch_shapes=[
             local,
             local,
@@ -691,7 +686,7 @@
             flat,
             stack,
             flat,
-            pltpu.VMEM((utts, frames * width // LOW, LOW), bf16),
+            stack,
             pltpu.VMEM((n_seq, rows_each, tokens, PICK_TILE), bf16),
             pltpu.VMEM((32, width), f32),
             partial,
@@ -699,6 +694,10 @@
             pltpu.VMEM((held_rows, 128), f32),
             pltpu.VMEM((n_dp, held_rows, 128), f32),
             partial,
+            pltpu.VMEM((8, 128), f32),
+            pltpu.VMEM((n_seq, 8, 128), f32),
+            pltpu.VMEM((8, 128), f32),
+            pltpu.VMEM((n_dp, 8, 128), f32),
             pltpu.SemaphoreType.DMA((6,)),
             utt_sems,
             utt_sems,
@@ -712,6 +711,10 @@
             dp_sems,
             seq_sems,
             seq_sems,
+            seq_sems,
+            seq_sems,
+            dp_sems,
+            dp_sems,
         ],
         compiler_params=pltpu.CompilerParams(
             collective_id=2, has_side_effects=True, vmem_limit_bytes=56 * 2**20
@@ -727,10 +730,9 @@
         conv_cotangent,
         out_weight,
     )
-    conv_out, context_grad, total = written(conv_out, context_grad, total)
     flat_total = total.reshape(-1)
     weight_picks = flat_total[: pick_weight.shape[0]]
-    kernel_picks = flat_total[kernel_start : kernel_start + pick_kernel.shape[0]]
+    kernel_picks = tile.reshape(-1)[: pick_kernel.shape[0]]
     return (conv_out, context_grad, weight_picks, kernel_picks)
 
 

time: 123 us -> 87.6 us (0.71)
  Pallas kernels: 119 us -> 78.8 us
  local copies, waits for them, and re-layouts: 1.27 us -> 6.32 us
    pallas_call x1 -> x0, Pallas kernels: 27.9 us -> none  [written(): pl.pallas_call(write_kernel, out_shape=[jax.ShapeDtypeStruct(array.shape,...]
    pallas_call x1, Pallas kernels: 91.5 us -> 78.8 us  [one_kernel(): pl.pallas_call(functools.partial(block_kernel, n_seq, n_dp, rows_each, sc...]
    unnamed x0 -> x3, local copies, waits for them, and re-layouts: none -> 5.07 us
where the time goes in v4:
time: 87.6 us; the launch traced here: 87.3 us
  Pallas kernels  78.8 us (90%)
  local copies, waits for them, and re-layouts  6.32 us (7%)
  other arithmetic  1.56 us (2%)
    pallas_call x1, Pallas kernels, one_kernel(): pl.pallas_call(functools.partial(block_kernel, n_seq, n_dp, rows_each, sc...  78.8 us
    unnamed x3, local copies, waits for them, and re-layouts  5.07 us

profile of v4, /device:TPU:0, one launch (start us, length us, event | category | flops | bytes accessed | tf_op | source)
XLA Modules:
  0.0 87.3 jit_solution(6274589565702449783)
XLA Ops:
  0.6 1.6 %pad_add_fusion = s32[24576]{0:T(1024)} fusion(s32[476]{0:T(512)} %param.19, s32[23592]{0:T(1024)} %param.18), kind=kLoop, calls=%fused_computation | loop fusion | flops 24576 | bytes 194576 | tf_op jit(solution)/shard_map/concatenate | solution.py:638
  2.2 78.8 %shard_map.129 = (bf16[2,64,1536]{2,1,0:T(8,128)(2,1)}, bf16[2,64,1536]{2,1,0:T(8,128)(2,1)}, f32[192,128]{1,0:T(8,128)}, f32[8,128]{1,0:T(8,128)}) custom-call(s32[2]{0:T(128)} %len_ref.1, s32[8,24,128]{2,1,0:T(8,128)} %bitcast.4, bf16[31,1536]{1,0:T(8,128)(2,1)} %kern_ref.1, bf16[2,64,1536]{2,1,0:T(8,128)(2,1)} %q_hbm.1, bf16[2,64,1536]{2,1,0:T(8,128)(2,1)} %k_hbm.1, ...), custom_call_target="tpu_custom_call" | custom-call | tf_op jit(solution)/shard_map/pallas_call | solution.py:660
  81.0 1.3 %slice.7 = f32[476]{0:T(512)} slice(f32[1024]{0:T(1024)} %bitcast.6), slice={[0:476]} | slice | bytes 3808 | tf_op jit(solution)/shard_map/slice | solution.py:735
  82.2 1.8 %copy.17 = bf16[2,64,1536]{2,1,0:T(8,128)(2,1)} copy(bf16[2,64,1536]{2,1,0:T(8,128)(2,1)} %get-tuple-element.16) | data formatting | bytes 786432
  84.0 1.8 %copy.18 = bf16[2,64,1536]{2,1,0:T(8,128)(2,1)} copy(bf16[2,64,1536]{2,1,0:T(8,128)(2,1)} %get-tuple-element.17) | data formatting | bytes 786432
  85.8 1.5 %copy.19 = f32[23592]{0:T(1024)} copy(f32[23592]{0:T(1024)} %bitcast.5) | data formatting | bytes 188736

commit v5 on v4

--- a/solution.py
+++ b/solution.py
@@ -152,6 +152,39 @@
     for part in range(1, stacked.shape[0] // tokens):
         out = jnp.where(high == part, every[part * tokens : (part + 1) * tokens], out)
     return out
+
+
+GROUP = 16
+
+
+def one_hot(low):
+    ids = lax.broadcasted_iota(jnp.int32, (LOW, low.shape[1]), 0).astype(jnp.bfloat16)
+    one, zero = jnp.bfloat16(1.0), jnp.bfloat16(0.0)
+    return jnp.where(ids == low.astype(jnp.bfloat16), one, zero)
+
+
+def choose_groups(stacked, tokens, index):
+    parts = stacked.shape[0] // tokens
+    high = lax.div(index, LOW)
+    every = jnp.dot(
+        stacked, one_hot(lax.rem(index, LOW)), preferred_element_type=jnp.float32
+    )
+    for group in range(tokens // GROUP):
+        begin = group * parts * GROUP
+        out = every[begin : begin + GROUP]
+        for part in range(1, parts):
+            place = begin + part * GROUP
+            out = jnp.where(high == part, every[place : place + GROUP], out)
+        yield group * GROUP, out
+
+
+def stack_groups(stack, rows, first_row, parts):
+    for group in range(rows.shape[0] // GROUP):
+        for part in range(parts):
+            begin = (first_row // GROUP + group) * parts * GROUP + part * GROUP
+            stack[begin : begin + GROUP, :] = rows[
+                group * GROUP : (group + 1) * GROUP, part * LOW : (part + 1) * LOW
+            ]
 
 
 def picks_kernel(pick_ref, ctx_ref, grad_ref, out_ref, ctx_stack, grad_stack):
@@ -435,18 +468,19 @@
             hid_pad[utt, reach : reach + frames, cols] = value.astype(jnp.float32)
 
         sent = swap_edges(hidden, hid_edge, utt, 2 * utts + 2 * utt)
-        for part in range(width // LOW):
-            begin = part * tokens + first_row
-            ctx_stack[begin : begin + frames, :] = ctx[rows, part * LOW : (part + 1) * LOW]
+        stack_groups(ctx_stack, ctx[rows, :], first_row, width // LOW)
         return sent
 
     def pick_context():
         @pl.loop(0, n_seq)
         def _(owner):
             for row in range(rows_each):
-                found = choose(ctx_stack[...], tokens, lax.div(pick_row(owner, row), width))
-                found = found * grad_picked[owner, row].astype(jnp.float32)
-                store_row(x_ref.at[owner], row, jnp.sum(found, axis=0, keepdims=True))
+                index = lax.div(pick_row(owner, row), width)
+                total = jnp.zeros((GROUP, PICK_TILE), jnp.float32)
+                for begin, found in choose_groups(ctx_stack[...], tokens, index):
+                    other = grad_picked[owner, row, begin : begin + GROUP, :]
+                    total = total + found * other.astype(jnp.float32)
+                store_row(x_ref.at[owner], row, jnp.sum(total, axis=0, keepdims=True))
 
     def pick_row(owner, row):
         return jnp.concatenate(
@@ -485,17 +519,15 @@
             total = jnp.where(frame_ids < len_ref[utt], total, 0.0)
             grad[utt * frames : (utt + 1) * frames, cols] = total.astype(jnp.bfloat16)
 
-    for part in range(width // LOW):
-        grad_stack[part * tokens : (part + 1) * tokens, :] = grad[
-            :, part * LOW : (part + 1) * LOW
-        ]
+    stack_groups(grad_stack, grad[...], 0, width // LOW)
 
     def pick_grad(begin, end):
         @pl.loop(begin, end)
         def _(owner):
             for row in range(rows_each):
-                found = choose(grad_stack[...], tokens, lax.rem(pick_row(owner, row), width))
-                grad_picked[owner, row] = found.astype(jnp.bfloat16)
+                index = lax.rem(pick_row(owner, row), width)
+                for begin, found in choose_groups(grad_stack[...], tokens, index):
+                    grad_picked[owner, row, begin : begin + GROUP, :] = found.astype(jnp.bfloat16)
 
     for utt in range(1, utts):
         copies += send_heads(utt)
@@ -604,7 +636,7 @@
     convolve(third_part, width // 128)
     for copy in tile_second:
         copy.wait_recv()
-    tile_ref[...] = jnp.sum(tile_sums[...], axis=0) * norm_factor
+    tile_ref[...] = jnp.sum(tile_sums[...], axis=0)[: tile_ref.shape[0]] * norm_factor
     for copy in third:
         copy.wait_recv()
     for owner in range(n_seq):
@@ -613,6 +645,34 @@
         copy.wait_send()
     for copy in tile_first + tile_second:
         copy.wait_send()
+
+
+def write_kernel(count, *refs):
+    sources, outs, held = refs[:count], refs[count : 2 * count], refs[2 * count : 3 * count]
+    in_sems, out_sems = refs[3 * count :]
+    reads = [pltpu.make_async_copy(sources[i], held[i], in_sems.at[i]) for i in range(count)]
+    writes = [pltpu.make_async_copy(held[i], outs[i], out_sems.at[i]) for i in range(count)]
+    for copy in reads:
+        copy.start()
+    for read, write in zip(reads, writes):
+        read.wait()
+        write.start()
+    for copy in writes:
+        copy.wait()
+
+
+def written(*arrays):
+    spec = pl.BlockSpec(memory_space=pl.ANY)
+    count = len(arrays)
+    sems = pltpu.SemaphoreType.DMA((count,))
+    return pl.pallas_call(
+        functools.partial(write_kernel, count),
+        out_shape=[jax.ShapeDtypeStruct(array.shape, array.dtype) for array in arrays],
+        in_specs=[spec] * count,
+        out_specs=[spec] * count,
+        scratch_shapes=[pltpu.VMEM(array.shape, array.dtype) for array in arrays] + [sems, sems],
+        compiler_params=pltpu.CompilerParams(vmem_limit_bytes=56 * 2**20),
+    )(*arrays)
 
 
 def one_kernel(
@@ -663,7 +723,7 @@
             jax.ShapeDtypeStruct(queries.shape, bf16),
             jax.ShapeDtypeStruct(queries.shape, bf16),
             jax.ShapeDtypeStruct((n_seq * held_rows, 128), f32),
-            jax.ShapeDtypeStruct((8, 128), f32),
+            jax.ShapeDtypeStruct((PICK_TILE // 128, 128), f32),
         ),
         in_specs=[pl.BlockSpec(memory_space=pltpu.SMEM), vmem, vmem] + [hbm] * 6,
         out_specs=(vmem, vmem, vmem, vmem),
@@ -730,6 +790,7 @@
         conv_cotangent,
         out_weight,
     )
+    conv_out, context_grad, total, tile = written(conv_out, context_grad, total, tile)
     flat_total = total.reshape(-1)
     weight_picks = flat_total[: pick_weight.shape[0]]
     kernel_picks = tile.reshape(-1)[: pick_kernel.shape[0]]

time: 87.6 us -> 83.1 us (0.949)
  local copies, waits for them, and re-layouts: 6.32 us -> 0 us
  Pallas kernels: 78.8 us -> 80.7 us
    unnamed x3 -> x0, local copies, waits for them, and re-layouts: 5.07 us -> none
    pallas_call x0 -> x1, Pallas kernels: none -> 1.97 us  [written(): pl.pallas_call(functools.partial(write_kernel, count), out_shape=[jax.Sha...]
    slice x1 -> x0, local copies, waits for them, and re-layouts: 1.25 us -> none  [one_kernel(): kernel_picks = tile.reshape(-1)[:pick_kernel.shape[0]]]
where the time goes in v5:
time: 83.1 us; the launch traced here: 82.9 us
  Pallas kernels  80.7 us (97%)
  other arithmetic  1.56 us (2%)
    pallas_call x1, Pallas kernels, one_kernel(): pl.pallas_call(functools.partial(block_kernel, n_seq, n_dp, rows_each, sc...  78.8 us
    pallas_call x1, Pallas kernels, written(): pl.pallas_call(functools.partial(write_kernel, count), out_shape=[jax.Sha...  1.97 us

profile of v5, /device:TPU:0, one launch (start us, length us, event | category | flops | bytes accessed | tf_op | source)
XLA Modules:
  0.0 82.9 jit_solution(13867721621384103331)
XLA Ops:
  0.6 1.6 %pad_add_fusion = s32[24576]{0:T(1024)} fusion(s32[476]{0:T(512)} %param.19, s32[23592]{0:T(1024)} %param.18), kind=kLoop, calls=%fused_computation | loop fusion | flops 24576 | bytes 194576 | tf_op jit(solution)/shard_map/concatenate | solution.py:698
  2.2 78.8 %shard_map.129 = (bf16[2,64,1536]{2,1,0:T(8,128)(2,1)}, bf16[2,64,1536]{2,1,0:T(8,128)(2,1)}, f32[192,128]{1,0:T(8,128)}, f32[4,128]{1,0:T(4,128)}) custom-call(s32[2]{0:T(128)} %len_ref.1, s32[8,24,128]{2,1,0:T(8,128)} %bitcast.5, bf16[31,1536]{1,0:T(8,128)(2,1)} %kern_ref.1, bf16[2,64,1536]{2,1,0:T(8,128)(2,1)} %q_hbm.1, bf16[2,64,1536]{2,1,0:T(8,128)(2,1)} %k_hbm.1, ...), custom_call_target="tpu_custom_call" | custom-call | tf_op jit(solution)/shard_map/pallas_call | solution.py:720
  81.0 2.0 %shard_map.130 = (bf16[2,64,1536]{2,1,0:T(8,128)(2,1)}, bf16[2,64,1536]{2,1,0:T(8,128)(2,1)}, f32[192,128]{1,0:T(8,128)}, f32[4,128]{1,0:T(4,128)}) custom-call(bf16[2,64,1536]{2,1,0:T(8,128)(2,1)} %get-tuple-element.12.refs_0_, bf16[2,64,1536]{2,1,0:T(8,128)(2,1)} %get-tuple-element.13.refs_1_, f32[192,128]{1,0:T(8,128)} %get-tuple-element.14.refs_2_, ...), custom_call_target="tpu_custom_call" | custom-call | tf_op jit(solution)/shard_map/pallas_call | solution.py:668

commit v6 on v5

--- a/solution.py
+++ b/solution.py
@@ -471,16 +471,25 @@
         stack_groups(ctx_stack, ctx[rows, :], first_row, width // LOW)
         return sent
 
-    def pick_context():
-        @pl.loop(0, n_seq)
-        def _(owner):
-            for row in range(rows_each):
-                index = lax.div(pick_row(owner, row), width)
-                total = jnp.zeros((GROUP, PICK_TILE), jnp.float32)
-                for begin, found in choose_groups(ctx_stack[...], tokens, index):
-                    other = grad_picked[owner, row, begin : begin + GROUP, :]
-                    total = total + found * other.astype(jnp.float32)
-                store_row(x_ref.at[owner], row, jnp.sum(total, axis=0, keepdims=True))
+    def pick_context(owner):
+        for row in range(rows_each):
+            index = lax.div(pick_row(owner, row), width)
+            total = jnp.zeros((GROUP, PICK_TILE), jnp.float32)
+            for begin, found in choose_groups(ctx_stack[...], tokens, index):
+                other = grad_picked[owner, row, begin : begin + GROUP, :]
+                total = total + found * other.astype(jnp.float32)
+            store_row(x_ref.at[owner], row, jnp.sum(total, axis=0, keepdims=True))
+
+    def kernel_part(step):
+        cols = pl.ds(pl.multiple_of(step * 128, 128), 128)
+        found = {}
+        for utt in range(utts):
+            cot = cot_pad[utt, reach : reach + frames, cols]
+            for offset, window in shifted_windows(hid_pad[utt, :, cols], frames):
+                value = jnp.sum((window * cot).reshape(frames // 8, 8, 128), axis=0)
+                found[offset] = value if utt == 0 else found[offset] + value
+        for offset, value in found.items():
+            kern_grad[offset - 1 : offset, cols] = jnp.sum(value, axis=0, keepdims=True)
 
     def pick_row(owner, row):
         return jnp.concatenate(
@@ -554,28 +563,34 @@
         for copy in returns[utt * (n_seq - 1) : (utt + 1) * (n_seq - 1)]:
             copy.wait_recv()
         hid_copies += project(utt)
-    pick_context()
+    kern_grad[...] = jnp.zeros_like(kern_grad)
+    alone = n_seq // 2
+    rounds = n_seq - alone
+    steps = width // 128
+
+    @pl.loop(0, alone)
+    def _(owner):
+        pick_context(owner)
+
+    for copy in hid_copies:
+        copy.wait_recv()
+    pad_edges(hid_edge, hid_pad)
+
+    @pl.loop(0, rounds)
+    def _(turn):
+        pick_context(alone + turn)
+        for i in range(steps // rounds):
+            kernel_part(turn * (steps // rounds) + i)
+
     first = [
         send_to(x_ref.at[peer], parts.at[me], s1.at[i], r1.at[i], "seq", peer)
         for i, peer in enumerate(peers_of("seq", n_seq))
     ]
     parts[pl.ds(me, 1)] = x_ref[pl.ds(me, 1)]
-    for copy in hid_copies:
-        copy.wait_recv()
-    pad_edges(hid_edge, hid_pad)
-    kern_grad[...] = jnp.zeros_like(kern_grad)
-
-    @pl.loop(0, width // 128)
+
+    @pl.loop(steps // rounds * rounds, steps)
     def _(step):
-        cols = pl.ds(pl.multiple_of(step * 128, 128), 128)
-        found = {}
-        for utt in range(utts):
-            cot = cot_pad[utt, reach : reach + frames, cols]
-            for offset, window in shifted_windows(hid_pad[utt, :, cols], frames):
-                value = jnp.sum((window * cot).reshape(frames // 8, 8, 128), axis=0)
-                found[offset] = value if utt == 0 else found[offset] + value
-        for offset, value in found.items():
-            kern_grad[offset - 1 : offset, cols] = jnp.sum(value, axis=0, keepdims=True)
+        kernel_part(step)
 
     pick = pick_row(n_seq - 1, rows_each - 1)
     rest = jnp.concatenate(

time: 83.1 us -> 87.1 us (1.048)
  Pallas kernels: 80.7 us -> 84.7 us
    pallas_call x1, Pallas kernels: 78.8 us -> 82.7 us  [one_kernel(): pl.pallas_call(functools.partial(block_kernel, n_seq, n_dp, rows_each, sc...]
where the time goes in v6:
time: 87.1 us; the launch traced here: 86.9 us
  Pallas kernels  84.7 us (97%)
  other arithmetic  1.56 us (2%)
    pallas_call x1, Pallas kernels, one_kernel(): pl.pallas_call(functools.partial(block_kernel, n_seq, n_dp, rows_each, sc...  82.7 us
    pallas_call x1, Pallas kernels, written(): pl.pallas_call(functools.partial(write_kernel, count), out_shape=[jax.Sha...  1.97 us

profile of v6, /device:TPU:0, one launch (start us, length us, event | category | flops | bytes accessed | tf_op | source)
XLA Modules:
  0.0 86.9 jit_solution(3072941379551740936)
XLA Ops:
  0.6 1.6 %pad_add_fusion = s32[24576]{0:T(1024)} fusion(s32[476]{0:T(512)} %param.19, s32[23592]{0:T(1024)} %param.18), kind=kLoop, calls=%fused_computation | loop fusion | flops 24576 | bytes 194576 | tf_op jit(solution)/shard_map/concatenate | solution.py:713
  2.2 82.7 %shard_map.129 = (bf16[2,64,1536]{2,1,0:T(8,128)(2,1)}, bf16[2,64,1536]{2,1,0:T(8,128)(2,1)}, f32[192,128]{1,0:T(8,128)}, f32[4,128]{1,0:T(4,128)}) custom-call(s32[2]{0:T(128)} %len_ref.1, s32[8,24,128]{2,1,0:T(8,128)} %bitcast.5, bf16[31,1536]{1,0:T(8,128)(2,1)} %kern_ref.1, bf16[2,64,1536]{2,1,0:T(8,128)(2,1)} %q_hbm.1, bf16[2,64,1536]{2,1,0:T(8,128)(2,1)} %k_hbm.1, ...), custom_call_target="tpu_custom_call" | custom-call | tf_op jit(solution)/shard_map/pallas_call | solution.py:735
  84.9 2.0 %shard_map.130 = (bf16[2,64,1536]{2,1,0:T(8,128)(2,1)}, bf16[2,64,1536]{2,1,0:T(8,128)(2,1)}, f32[192,128]{1,0:T(8,128)}, f32[4,128]{1,0:T(4,128)}) custom-call(bf16[2,64,1536]{2,1,0:T(8,128)(2,1)} %get-tuple-element.12.refs_0_, bf16[2,64,1536]{2,1,0:T(8,128)(2,1)} %get-tuple-element.13.refs_1_, f32[192,128]{1,0:T(8,128)} %get-tuple-element.14.refs_2_, ...), custom_call_target="tpu_custom_call" | custom-call | tf_op jit(solution)/shard_map/pallas_call | solution.py:683
